TPU v7x, 256 devices: a whole 4x4x8 slice. The times are simulated.
256 devices in a mesh: dp: 16 (over z_hi, x, core), tensor: 16 (over z_lo, y).
Axes of the slice: x: 4, y: 4, z: 8 (z_hi: 2, z_lo: 4; z = z_hi * 4 + z_lo), core: 2. Of those that a mesh axis runs over, the one named last changes fastest.
Arguments:
- inputs: bfloat16 [6144, 2560], P(('dp', 'tensor')), may hold values from -6 to 6
- norm_gain: float32 [2560], replicated, may hold values from 0.5 to 1.5
- w_up: bfloat16 [2560, 10240], P(None, 'tensor'), may hold values from -0.07905694 to 0.07905694
- w_down: bfloat16 [10240, 2560], P('tensor'), may hold values from -0.0625 to 0.0625
- grad_out: bfloat16 [6144, 2560], P(('dp', 'tensor')), may hold values from -7 to 7
Outputs:
- output: bfloat16 [6144, 2560], P(('dp', 'tensor'))
- grad_in: bfloat16 [6144, 2560], P(('dp', 'tensor'))
- grad_up: bfloat16 [2560, 10240], P(None, 'tensor')
- grad_down: bfloat16 [10240, 2560], P('tensor')
- grad_gain: float32 [2560], replicated
All inputs are finite; a program needn't handle non-finite values.
Results may differ from a plain program's by a relative error of at most 0.024.
Values may be sent and summed in bfloat16 or wider, within the bound.
A program may use at most 192 MiB of HBM per device.

v0:
```python
import math

import jax
import jax.numpy as jnp
from jax import lax
from jax.sharding import PartitionSpec as P

BLOCK = 16


TWO_PI = 2.0 * math.pi
CONTRACT_ROWS = (((0,), (0,)), ((), ()))
CONTRACT_COLS = (((1,), (1,)), ((), ()))


def staircase(values):
    return values - jnp.sin(TWO_PI * values) / TWO_PI


def block_peak(values):
    row_count, col_count = values.shape
    block_max = jnp.max(jnp.abs(values).reshape(row_count, col_count // BLOCK, BLOCK), axis=2)
    return jnp.repeat(block_max, BLOCK, axis=1)


def per_device(inputs, norm_gain, w_up, w_down, grad_out):
    widened = inputs.astype(jnp.float32)
    inverse = lax.rsqrt(jnp.mean(widened * widened, axis=1, keepdims=True) + 1e-05)
    normed = widened * inverse * norm_gain
    x_scale = jnp.maximum(block_peak(normed), 1.5) / 6.0
    quantized = (x_scale * staircase(normed / x_scale)).astype(jnp.bfloat16)
    gathered = lax.all_gather(quantized, "tensor", axis=0, tiled=True)
    pre_act = jnp.dot(gathered, w_up, preferred_element_type=jnp.float32)
    active = jnp.maximum(pre_act, 0.0)
    hidden = active * active
    peak_value = lax.pmax(jnp.max(hidden), "tensor") + 1e-06
    h_scale = jnp.maximum(block_peak(hidden), peak_value / 8.0) / 6.0
    hidden_q = (h_scale * staircase(hidden / h_scale)).astype(jnp.bfloat16)
    picked = hidden_q
    output = lax.psum_scatter(
        jnp.dot(picked, w_down, preferred_element_type=jnp.float32).astype(jnp.bfloat16),
        "tensor",
        scatter_dimension=0,
        tiled=True,
    )
    cotangent = lax.all_gather(grad_out, "tensor", axis=0, tiled=True)
    down_part = lax.dot_general(
        hidden_q, cotangent, CONTRACT_ROWS, preferred_element_type=jnp.float32
    )
    down_sum = None
    grad_hq = lax.dot_general(cotangent, w_down, CONTRACT_COLS, preferred_element_type=jnp.float32)
    grad_z = (grad_hq * 2.0 * active).astype(jnp.bfloat16)
    picked = grad_z
    grad_xq = lax.psum_scatter(
        lax.dot_general(picked, w_up, CONTRACT_COLS, preferred_element_type=jnp.float32).astype(
            jnp.bfloat16
        ),
        "tensor",
        scatter_dimension=0,
        tiled=True,
    ).astype(jnp.float32)
    grad_gain = lax.psum(jnp.sum(grad_xq * widened * inverse, axis=0), ("dp", "tensor"))
    scaled = grad_xq * norm_gain
    cubed = inverse * inverse * inverse
    grad_in = (
        inverse * scaled - widened * cubed * jnp.mean(scaled * widened, axis=1, keepdims=True)
    ).astype(jnp.bfloat16)
    up_part = lax.dot_general(gathered, grad_z, CONTRACT_ROWS, preferred_element_type=jnp.float32)
    up_sum, down_sum = (
        lax.psum(up_part.astype(jnp.bfloat16), "dp").astype(jnp.float32),
        lax.psum(down_part.astype(jnp.bfloat16), "dp").astype(jnp.float32),
    )
    return (output, grad_in, up_sum.astype(jnp.bfloat16), down_sum.astype(jnp.bfloat16), grad_gain)


def solution(mesh):
    return jax.shard_map(
        per_device,
        mesh=mesh,
        in_specs=(
            P(("dp", "tensor"), None),
            P(),
            P(None, "tensor"),
            P("tensor", None),
            P(("dp", "tensor"), None),
        ),
        out_specs=(
            P(("dp", "tensor"), None),
            P(("dp", "tensor"), None),
            P(None, "tensor"),
            P("tensor", None),
            P(),
        ),
        check_vma=False,
    )
```

profile of v0, /device:TPU:1, one launch (start us, length us, event | category | flops | bytes accessed | tf_op | source)
XLA Modules:
  0.0 594.9 jit_solution(18340379943486654333)
XLA Ops:
  7.2 0.0 copy-start
  7.2 0.0 all-gather.3.cloned.1.call-start
  7.2 1.2 fusion.5
  8.4 1.0 fusion.8
  9.4 1.9 reshape.45
  11.4 0.0 copy-start.2
  11.4 0.0 copy-start.5
  11.4 2.5 reduce_max.27
  13.9 1.8 broadcast_in_dim.4
  15.7 3.6 div.40
  19.4 0.0 copy-done.2
  19.4 0.0 copy-done.5
  19.4 2.5 multiply_convert_fusion.1
  21.9 0.0 all-gather.3.cloned.1.call-update
  21.9 0.0 all-gather.5.cloned.1.call-start
  22.0 0.7 all-gather.5.cloned.1.call-update
  22.7 0.0 reduce-scatter.5.cloned.1.call-start
  22.7 76.0 %all-gather.3.cloned.1.call-done = bf16[384,2560]{1,0:T(8,128)(2,1)} async-done(((bf16[24,2560]{1,0:T(8,128)(2,1)}), bf16[384,2560]{1,0:T(8,128)(2,1)}) %all-gather.3.cloned.1.call-update) | async-done | bytes 1966096 | tf_op jit(solution)/shard_map/all_gather | solution.py:32
  98.8 0.0 copy-done
  98.8 5.1 multiply_reduce_fusion
  103.8 78.2 %all-gather.5.cloned.1.call-done = bf16[384,2560]{1,0:T(8,128)(2,1)} async-done(((bf16[24,2560]{1,0:T(8,128)(2,1)}), bf16[384,2560]{1,0:T(8,128)(2,1)}) %all-gather.5.cloned.1.call-update) | async-done | bytes 1966096 | tf_op jit(solution)/shard_map/all_gather | solution.py:46
  182.1 4.5 fusion.1
  186.6 0.0 copy-start.7
  186.6 0.8 copy-done.7
  187.3 3.0 convolution_convert_fusion.2
  190.4 0.0 reduce-scatter.5.cloned.1.call-update
  190.4 0.0 reduce-scatter.3.cloned.1.call-start
  190.5 37.6 %pmax.7 = f32[]{:T(128)} all-reduce(f32[]{:T(128)} %get-tuple-element.9), channel_id=1, replica_groups=mesh['dp'=16,'tensor'=16] {'tensor'}, use_global_device_ids=true, to_apply=%region_4.0 | all-reduce | flops 1 | bytes 8 | tf_op jit(solution)/shard_map/pmax | solution.py:36
  228.0 2.5 copy.10
  230.5 1.4 reduce_max.28
  232.6 1.0 broadcast_in_dim.5
  233.6 2.5 copy.12
  236.1 4.6 multiply_convert_fusion
  240.6 0.0 copy-start.3
  240.7 0.8 copy-done.3
  241.4 5.0 convolution_convert_fusion.3
  246.4 0.0 reduce-scatter.3.cloned.1.call-update
  246.4 0.2 all-reduce.3.cloned.1.call-start
  246.6 0.0 copy-start.4
  246.7 0.0 copy-start.6
  246.7 5.6 convolution_convert_fusion.1
  252.2 0.0 copy-done.4
  252.2 0.0 copy-done.6
  252.2 3.6 convolution_convert_fusion
  255.9 0.0 all-reduce.3.cloned.1.call-update
  255.9 20.6 %reduce-scatter.5.cloned.1.call-done = bf16[24,2560]{1,0:T(8,128)(2,1)} async-done(((bf16[384,2560]{1,0:T(8,128)(2,1)}), bf16[24,2560]{1,0:T(8,128)(2,1)}) %reduce-scatter.5.cloned.1.call-update) | async-done | bytes 122896 | tf_op jit(solution)/shard_map/reduce_scatter | solution.py:54
  276.5 1.1 fusion.12
  277.6 85.9 %psum.23 = f32[2560]{0:T(1024)} all-reduce(f32[2560]{0:T(1024)S(1)} %get-tuple-element.5), channel_id=1, replica_groups=mesh['dp'=16,'tensor'=16] {'dp','tensor'}, use_global_device_ids=true, to_apply=%region_11.0 | all-reduce | flops 2560 | bytes 20480 | tf_op jit(solution)/shard_map/psum | solution.py:62
  363.5 1.7 fusion.4
  365.2 0.0 reduce-scatter.3.cloned.1.call-done
  365.2 217.4 %all-reduce.3.cloned.1.call-done = (bf16[2560,640]{1,0:T(8,128)(2,1)}, bf16[640,2560]{1,0:T(8,128)(2,1)}) async-done(((bf16[2560,640]{1,0:T(8,128)(2,1)}, bf16[640,2560]{1,0:T(8,128)(2,1)}), (bf16[2560,640]{1,0:T(8,128)(2,1)}, bf16[640,2560]{1,0:T(8,128)(2,1)})) %all-reduce.3.cloned.1.call-update) | async-done | bytes 6553616 | tf_op jit(solution)/shard_map/psum | solution.py:70
  582.6 0.0 copy-start.1
  582.6 4.1 copy.15
  586.6 0.0 copy-done.1
  586.6 1.7 copy.16
  (4 shorter events, 0.0 us)
Async XLA Ops:
  7.2 91.6 %copy-start = (bf16[2560,640]{1,0:T(8,128)(2,1)S(1)}, bf16[2560,640]{1,0:T(8,128)(2,1)}, u32[]{:S(2)}) copy-start(bf16[2560,640]{1,0:T(8,128)(2,1)} %param.7) | copy-start | bytes 9830404
  7.2 91.6 %all-gather.3.cloned.1.call-start = ((), (), s32[]{:S(2)}) async-start(), calls=%async_computation.2 | async-start | bytes 2088960 | tf_op jit(solution)/shard_map/all_gather | solution.py:32
  11.4 8.0 %copy-start.2 = (bf16[24,2560]{1,0:T(8,128)(2,1)S(1)}, bf16[24,2560]{1,0:T(8,128)(2,1)}, u32[]{:S(2)}) copy-start(bf16[24,2560]{1,0:T(8,128)(2,1)} %param.5) | copy-start | bytes 368644
  11.4 8.0 %copy-start.5 = (f32[2560]{0:T(1024)S(1)}, f32[2560]{0:T(1024)}, u32[]{:S(2)}) copy-start(f32[2560]{0:T(1024)} %param.6) | copy-start | bytes 30724
  21.9 160.2 %all-gather.5.cloned.1.call-start = ((), (), s32[]{:S(2)}) async-start(), calls=%async_computation.4 | async-start | bytes 2088960 | tf_op jit(solution)/shard_map/all_gather | solution.py:46
  22.7 253.8 %reduce-scatter.5.cloned.1.call-start = ((), (), s32[]{:S(2)}) async-start(), calls=%async_computation.5 | async-start | bytes 2088960 | tf_op jit(solution)/shard_map/reduce_scatter | solution.py:54
  186.6 0.8 copy-start.7
  190.4 174.8 %reduce-scatter.3.cloned.1.call-start = ((), (), s32[]{:S(2)}) async-start(), calls=%async_computation.3 | async-start | bytes 2088960 | tf_op jit(solution)/shard_map/reduce_scatter | solution.py:40
  240.6 0.8 copy-start.3
  246.4 336.2 %all-reduce.3.cloned.1.call-start = ((), (), s32[]{:S(2)}) async-start(), calls=%async_computation.6 | async-start | bytes 13107200 | tf_op jit(solution)/shard_map/psum | solution.py:70
  246.6 5.6 copy-start.4
  246.7 5.6 copy-start.6
  582.6 4.1 copy-start.1
Sparse Core Ops, SparseCore 0:
  22.0 76.6 all-gather.2
  100.5 81.4 all-gather.4
  190.5 85.9 reduce-scatter.4
  279.6 83.5 reduce-scatter.2
  366.4 216.1 all-reduce.2
where the time goes:
time: 602 us; the launch traced here: 595 us
  waiting for transfers between devices  393 us (65%)
  blocking collectives  123 us (20%)
  matrix products  26.8 us (4%)
  local copies, waits for them, and re-layouts  20.8 us (3%)
  other arithmetic  15.9 us (3%)
  between operations  14.5 us (2%)
    psum x1, waiting for transfers between devices, per_device(): lax.psum(up_part.astype(jnp.bfloat16), 'dp').astype(jnp.float32)  217 us
    psum x1, blocking collectives, per_device(): lax.psum(jnp.sum(grad_xq * widened * inverse, axis=0), ('dp', 'tensor'))  85.9 us
    all_gather x1, waiting for transfers between devices, per_device(): cotangent = lax.all_gather(grad_out, 'tensor', axis=0, tiled=True)  78.2 us
    all_gather x1, waiting for transfers between devices, per_device(): gathered = lax.all_gather(quantized, 'tensor', axis=0, tiled=True)  76 us
    pmax x1, blocking collectives, per_device(): peak_value = lax.pmax(jnp.max(hidden), 'tensor') + 1e-06  37.6 us
    reduce_scatter x1, waiting for transfers between devices, per_device(): lax.psum_scatter(lax.dot_general(picked, w_up, CONTRACT_COLS, preferred_e...  20.6 us
  transfers between devices with their start and end apart: 5, of which 4 were waited for; matrix products, arithmetic and copies ran while one was open for 6% of the time, Pallas kernels for 0%

commit v1 on v0

v1 whole, which is shorter than its diff:
```python
import functools

import jax
import jax.numpy as jnp
from jax import lax
from jax.experimental import pallas as pl
from jax.experimental.pallas import tpu as pltpu
from jax.sharding import PartitionSpec as P

MESH = pl.DeviceIdType.MESH
F32 = jnp.float32
BF16 = jnp.bfloat16

D = 2560
F = 640
T = 384
R = 24
H = D // 2
N_SEM = 256

SINE = (
    0.9999999958410793,
    -6.579735564529717,
    12.987846451008128,
    -12.207473944175224,
    6.687349899038311,
    -2.367236060103434,
    0.5102235956366108,
)
NT = (((1,), (1,)), ((), ()))
NN = (((1,), (0,)), ((), ()))


def dot(a, b, dims=NN):
    return lax.dot_general(a, b, dims, preferred_element_type=F32)


def staircase(values):
    r = values - jnp.floor(values + 0.5)
    s = r * r
    p = jnp.full_like(s, SINE[-1])
    for c in SINE[-2::-1]:
        p = p * s + c
    return values - p * r


def block_peak(values):
    lane = lax.broadcasted_iota(jnp.int32, values.shape, 1)
    for s in (1, 2, 4, 8):
        up = pltpu.roll(values, s, 1)
        down = pltpu.roll(values, 128 - s, 1)
        values = jnp.maximum(values, jnp.where((lane & s) != 0, up, down))
    return values


def quantize(values, magnitude, floor):
    peak = jnp.maximum(block_peak(magnitude), floor)
    return peak * (1.0 / 6.0) * staircase(values * (6.0 / peak))


class Copies:
    def __init__(self, send, recv):
        self.send, self.recv, self.all = send, recv, []

    def start(self, src, dst, device):
        n = len(self.all)
        copy = pltpu.make_async_remote_copy(
            src_ref=src,
            dst_ref=dst,
            send_sem=self.send.at[n],
            recv_sem=self.recv.at[n],
            device_id=device,
            device_id_type=MESH,
        )
        copy.start()
        self.all.append(copy)
        return copy


def kernel(
    x_ref, gain_ref, wu_hbm, wd_hbm, go_ref,
    out_ref, gin_ref, gup_ref, gdn_ref, gg_ref,
    wu, wd, cg, qg, c2, q2, aa, ss, cc, ghq, pa, gz2, hq, ht,
    po, px, ro, rx, zo, zx, u, ur, uz, d, dr, dz,
    py, pz, gy, gzl, gx, gc, gh, gfull, send, recv, local,
):
    dp, tn = lax.axis_index("dp"), lax.axis_index("tensor")
    zh, x, c = dp // 8, (dp // 2) % 4, dp % 2
    zl, y = tn // 4, tn % 4

    def dev(zh=zh, x=x, c=c, zl=zl, y=y):
        return ((zh * 4 + x) * 2 + c, zl * 4 + y)

    def mod(v):
        return lax.rem(v + 8, 4)

    def block(yy, zz):
        return yy * 4 + zz

    yp, ym = dev(y=mod(y + 1)), dev(y=mod(y - 1))
    xp, xm = dev(x=mod(x + 1)), dev(x=mod(x - 1))
    other = dev(c=1 - c)
    zfar = dev(zh=1 - zh)
    y_peers = [dev(y=mod(y + k)) for k in (1, 2, 3)]
    z_peers = [dev(zl=mod(zl + k)) for k in (1, 2, 3)]
    x_peers = [dev(x=mod(x + k)) for k in (1, 2, 3)]
    copies = Copies(send, recv)
    go = copies.start

    load_up = pltpu.make_async_copy(wu_hbm, wu, local.at[0])
    load_up.start()
    load_down = pltpu.make_async_copy(wd_hbm, wd, local.at[1])
    load_down.start()

    barrier = pltpu.get_barrier_semaphore()
    peers = y_peers + z_peers + x_peers + [other, zfar]
    for peer in peers:
        pl.semaphore_signal(barrier, inc=1, device_id=peer, device_id_type=MESH)
    pl.semaphore_wait(barrier, len(peers))

    def gather_z(buf, src):
        at = buf.at[block(y, zl)]
        return [go(src, at, peer) for peer in z_peers]

    def gather_y(buf, k, src=None):
        at = buf.at[block(y, mod(zl - k))]
        src = at if src is None else src
        return go(src, at, yp), go(src, at, ym)

    def forward(buf, k, pair):
        plus, minus = pair
        zz = mod(zl - k)
        plus.wait_recv()
        at = buf.at[block(mod(y - 1), zz), :, pl.ds(0, H)]
        a = go(at, at, yp)
        minus.wait_recv()
        at = buf.at[block(mod(y + 1), zz), :, pl.ds(H, H)]
        b = go(at, at, ym)
        return a, b

    cz = gather_z(cg, go_ref)
    cy = [gather_y(cg, 0, go_ref)]
    cg[block(y, zl)] = go_ref[...]

    wide = x_ref[...].astype(F32)
    inverse = lax.rsqrt(jnp.mean(wide * wide, axis=1, keepdims=True) + 1e-05)
    for i in range(D // 128):
        cols = slice(i * 128, (i + 1) * 128)
        normed = wide[:, cols] * inverse * gain_ref[:, cols]
        q = quantize(normed, jnp.abs(normed), 1.5)
        qg[block(y, zl), :, cols] = q.astype(BF16)

    qz = gather_z(qg, qg.at[block(y, zl)])
    qy = [gather_y(qg, 0)]
    for k in (1, 2, 3):
        cz[k - 1].wait_recv()
        cy.append(gather_y(cg, k))
    cf = [forward(cg, k, cy[k]) for k in (0, 1)]
    for k in (1, 2, 3):
        qz[k - 1].wait_recv()
        qy.append(gather_y(qg, k))
    cf += [forward(cg, k, cy[k]) for k in (2, 3)]
    qf = [forward(qg, k, qy[k]) for k in (0, 1)]
    for pair in cf:
        for copy in pair:
            copy.wait_recv()

    @pl.loop(0, D // 256)
    def _(i):
        cols = pl.ds(pl.multiple_of(i * 256, 256), 256)
        c2[:, cols] = cg[:, :, cols].astype(F32).reshape(T, 256).astype(BF16)

    other_half = pl.ds(pl.multiple_of((1 - c) * H, H), H)
    own_half = pl.ds(pl.multiple_of(c * H, H), H)
    ccx = go(c2.at[:, other_half], cc.at[pl.ds(T, T), :], other)
    cc[pl.ds(0, T), :] = c2[:, own_half]

    qf += [forward(qg, k, qy[k]) for k in (2,)]
    load_down.wait()

    @pl.loop(0, 5)
    def _(i):
        ks = pl.ds(pl.multiple_of(i * 512, 512), 512)
        part = dot(c2[:, ks], wd[:, ks], NT)

        @pl.when(i == 0)
        def _():
            ghq[...] = part

        @pl.when(i > 0)
        def _():
            ghq[...] += part

    qf += [forward(qg, k, qy[k]) for k in (3,)]
    for pair in qf:
        for copy in pair:
            copy.wait_recv()

    def lay(i, start, put):
        cols = pl.ds(pl.multiple_of(start + i * 256, 256), 256)
        v = qg[:, :, cols].astype(F32).reshape(T, 256)
        q2[:, cols] = v.astype(BF16)
        put(pl.ds(pl.multiple_of(i * 256, 256), 256), v.T.astype(BF16))

    def put_other(rows, v):
        ss[rows, :] = v

    def put_own(rows, v):
        aa[rows, pl.ds(0, T)] = v

    @pl.loop(0, 5)
    def _(i):
        lay(i, (1 - c) * H, put_other)

    aax = go(ss, aa.at[:, pl.ds(T, T)], other)

    @pl.loop(0, 5)
    def _(i):
        lay(i, c * H, put_own)

    load_up.wait()

    @pl.loop(0, 5)
    def _(i):
        ks = pl.ds(pl.multiple_of(i * 512, 512), 512)
        part = dot(q2[:, ks], wu[ks, :])

        @pl.when(i == 0)
        def _():
            pa[...] = part

        @pl.when(i > 0)
        def _():
            pa[...] += part

    def grad_tile(i, most):
        rows = pl.ds(pl.multiple_of(i * 64, 64), 64)
        for j in range(F // 128):
            cols = slice(j * 128, (j + 1) * 128)
            active = jnp.maximum(pa[rows, cols], 0.0)
            pa[rows, cols] = active
            gz2[rows, cols] = (ghq[rows, cols] * 2.0 * active).astype(BF16)
            most = jnp.maximum(most, active)
        return most

    most = lax.fori_loop(0, T // 64, grad_tile, jnp.zeros((64, 128), F32))
    gzx = go(gz2.at[pl.ds(0, T)], gz2.at[pl.ds(T, T)], other)
    most = jnp.max(jnp.max(most, axis=0, keepdims=True), axis=1, keepdims=True)
    py[y] = jnp.broadcast_to(most * most, (8, 128))
    pyx = [go(py.at[y], py.at[y], peer) for peer in y_peers]

    class Ring:
        def __init__(self, pos, plus, minus, view, got, add):
            self.pos, self.to = pos, (plus, minus)
            self.view, self.got, self.add = view, got, add
            self.last = [None, None]

        def send(self, s, way):
            j = mod(self.pos - 1 - s) if way == 0 else mod(self.pos + 1 + s)
            at = self.view(j, way)
            self.last[way] = go(at, self.got.at[way, s], self.to[way])

        def take(self, s):
            for way in (0, 1):
                self.last[way].wait_recv()
                j = mod(self.pos - 2 - s) if way == 0 else mod(self.pos + 2 + s)
                self.add(j, way, s)
                if s < 2:
                    self.send(s + 1, way)

    def adder(view, got, tiles, cut):
        def add(j, way, s):
            mine, theirs = view(j, way), got.at[way, s]

            @pl.loop(0, tiles)
            def _(i):
                at = cut(i)
                mine[at] = (mine[at].astype(F32) + theirs[at].astype(F32)).astype(BF16)

        return add

    def rows_of(n):
        return lambda i: (pl.ds(pl.multiple_of(i * n, n), n), slice(None))

    def u_view(j, way):
        return u.at[j, way]

    def d_view(j, way):
        return d.at[j, way]

    def p_view(buf):
        return lambda j, way: buf.at[j, :, :, pl.ds(way * H, H)]

    up = Ring(x, xp, xm, u_view, ur, adder(u_view, ur, 5, rows_of(32)))
    down = Ring(x, xp, xm, d_view, dr, adder(d_view, dr, 5, rows_of(16)))
    out = Ring(y, yp, ym, p_view(po), ro, adder(p_view(po), ro, 4, lambda i: i))
    gin = Ring(y, yp, ym, p_view(px), rx, adder(p_view(px), rx, 4, lambda i: i))

    aax.wait_recv()
    gzx.wait_recv()

    def up_chunk(j):
        rows = pl.ds(pl.multiple_of(j * 320, 320), 320)
        u[j] = dot(aa[rows, :], gz2[...]).reshape(2, 160, F).astype(BF16)

    up_chunk(mod(x - 1))
    up.send(0, 0)
    up_chunk(mod(x + 1))
    up.send(0, 1)
    up_chunk(mod(x + 2))
    up_chunk(x)

    for copy in pyx:
        copy.wait_recv()
    peak = jnp.maximum(jnp.maximum(py[0], py[1]), jnp.maximum(py[2], py[3]))
    pz[zl] = peak
    pzx = [go(pz.at[zl], pz.at[zl], peer) for peer in z_peers]

    @pl.loop(0, 5)
    def _(i):
        ns = pl.ds(pl.multiple_of(i * 512, 512), 512)
        part = dot(gz2[pl.ds(0, T), :], wu[ns, :], NT)
        px[:, :, :, ns] = part.reshape(4, 4, R, 512).astype(BF16)

    gin.send(0, 0)
    gin.send(0, 1)

    for copy in pzx:
        copy.wait_recv()
    peak = jnp.maximum(jnp.maximum(pz[0], pz[1]), jnp.maximum(pz[2], pz[3]))
    floor = (peak[0:1, :] + 1e-06) * 0.125

    @pl.loop(0, T // 128)
    def _(i):
        rows = pl.ds(pl.multiple_of(i * 128, 128), 128)
        for j in range(F // 128):
            cols = slice(j * 128, (j + 1) * 128)
            active = pa[rows, cols]
            hidden = active * active
            q = quantize(hidden, hidden, floor)
            hq[rows, cols] = q.astype(BF16)
            ht[cols, rows] = q.T.astype(BF16)

    htx = go(ht.at[:, pl.ds(0, T)], ht.at[:, pl.ds(T, T)], other)
    up.take(0)

    @pl.loop(0, 5)
    def _(i):
        ns = pl.ds(pl.multiple_of(i * 512, 512), 512)
        part = dot(hq[...], wd[:, ns])
        po[:, :, :, ns] = part.reshape(4, 4, R, 512).astype(BF16)

    ccx.wait_recv()
    htx.wait_recv()

    def down_chunk(j):
        rows = pl.ds(pl.multiple_of(j * 160, 160), 160)
        d[j] = dot(ht[rows, :], cc[...]).reshape(2, 80, H).astype(BF16)

    down_chunk(mod(x - 1))
    down.send(0, 0)
    down_chunk(mod(x + 1))
    down.send(0, 1)
    out.send(0, 0)
    out.send(0, 1)
    down_chunk(mod(x + 2))
    down_chunk(x)

    gin.take(0)
    up.take(1)
    down.take(0)
    out.take(0)
    up.take(2)
    uzx = go(u.at[x], uz, zfar)
    gin.take(1)
    down.take(1)
    out.take(1)
    gin.take(2)

    def scatter_z(buf, got):
        return [
            go(buf.at[y, mod(zl + k)], got.at[k - 1], z_peers[k - 1]) for k in (1, 2, 3)
        ]

    gin_z = scatter_z(px, zx)
    down.take(2)
    dzx = go(d.at[x], dz, zfar)
    out.take(2)
    out_z = scatter_z(po, zo)

    for copy in gin_z:
        copy.wait_recv()

    def total(buf, got, cols):
        t = buf[y, zl, :, cols].astype(F32) + got[0, :, cols].astype(F32)
        return t + got[1, :, cols].astype(F32) + got[2, :, cols].astype(F32)

    dots = jnp.zeros((R, 128), F32)
    for i in range(D // 128):
        cols = slice(i * 128, (i + 1) * 128)
        g = total(px, zx, cols)
        w = x_ref[:, cols].astype(F32)
        gfull[:, cols] = g
        dots = dots + g * gain_ref[:, cols] * w
        gy[y, i : i + 1, :] = jnp.sum(g * w * inverse, axis=0, keepdims=True)
    gyx = [go(gy.at[y], gy.at[y], peer) for peer in y_peers]
    mean = jnp.sum(dots, axis=1, keepdims=True) * (1.0 / D)
    cubed = inverse * inverse * inverse * mean
    for i in range(D // 128):
        cols = slice(i * 128, (i + 1) * 128)
        w = x_ref[:, cols].astype(F32)
        gin_ref[:, cols] = (
            inverse * (gfull[:, cols] * gain_ref[:, cols]) - w * cubed
        ).astype(BF16)

    for copy in gyx:
        copy.wait_recv()
    gzl[zl] = gy[0] + gy[1] + gy[2] + gy[3]
    gzx2 = [go(gzl.at[zl], gzl.at[zl], peer) for peer in z_peers]

    def spread(own, chunk, buf, at_chunk, at_half):
        res = []
        at = buf.at[at_chunk(c, x)]
        res.append((go(at, at, xp), go(at, at, xm)))
        res.append(go(at, at, other))
        return res

    def up_rows(cc_, j, way=None):
        if way is None:
            return (pl.ds(pl.multiple_of(cc_ * H + j * 320, 320), 320), slice(None))
        start = cc_ * H + j * 320 + way * 160
        return (pl.ds(pl.multiple_of(start, 160), 160), slice(None))

    def down_rows(cc_, j, way=None):
        cols = pl.ds(pl.multiple_of(cc_ * H, H), H)
        if way is None:
            return (pl.ds(pl.multiple_of(j * 160, 160), 160), cols)
        return (pl.ds(pl.multiple_of(j * 160 + way * 80, 80), 80), cols)

    class Spread:
        def __init__(self, buf, where):
            self.buf, self.where = buf, where

        def begin(self):
            at = self.buf.at[self.where(c, x)]
            self.plus, self.minus = go(at, at, xp), go(at, at, xm)
            self.cross = [go(at, at, other)]

        def middle(self):
            self.plus.wait_recv()
            at = self.buf.at[self.where(c, mod(x - 1), 0)]
            self.fplus = go(at, at, xp)
            at = self.buf.at[self.where(c, mod(x - 1))]
            self.cross.append(go(at, at, other))
            self.minus.wait_recv()
            at = self.buf.at[self.where(c, mod(x + 1), 1)]
            self.fminus = go(at, at, xm)
            at = self.buf.at[self.where(c, mod(x + 1))]
            self.cross.append(go(at, at, other))

        def end(self):
            self.fplus.wait_recv()
            at = self.buf.at[self.where(c, mod(x + 2), 0)]
            self.cross.append(go(at, at, other))
            self.fminus.wait_recv()
            at = self.buf.at[self.where(c, mod(x + 2), 1)]
            self.cross.append(go(at, at, other))

        def finish(self):
            for copy in self.cross:
                copy.wait_recv()

    uzx.wait_recv()
    for way in (0, 1):
        gup_ref[up_rows(c, x, way)] = (
            u[x, way].astype(F32) + uz[way].astype(F32)
        ).astype(BF16)
    spread_up = Spread(gup_ref, up_rows)
    spread_up.begin()

    for copy in gzx2:
        copy.wait_recv()
    gx[x] = gzl[0] + gzl[1] + gzl[2] + gzl[3]
    gxx = [go(gx.at[x], gx.at[x], peer) for peer in x_peers]

    for copy in out_z:
        copy.wait_recv()
    for i in range(D // 128):
        cols = slice(i * 128, (i + 1) * 128)
        out_ref[:, cols] = total(po, zo, cols).astype(BF16)

    spread_up.middle()

    for copy in gxx:
        copy.wait_recv()
    gc[c] = gx[0] + gx[1] + gx[2] + gx[3]
    gcx = go(gc.at[c], gc.at[c], other)

    dzx.wait_recv()
    for way in (0, 1):
        gdn_ref[down_rows(c, x, way)] = (
            d[x, way].astype(F32) + dz[way].astype(F32)
        ).astype(BF16)
    spread_down = Spread(gdn_ref, down_rows)
    spread_down.begin()

    gcx.wait_recv()
    gh[zh] = gc[0] + gc[1]
    ghx = go(gh.at[zh], gh.at[zh], zfar)
    spread_up.end()
    ghx.wait_recv()
    gg_ref[...] = gh[0] + gh[1]
    spread_down.middle()
    spread_down.end()
    spread_up.finish()
    spread_down.finish()
    for copy in copies.all:
        copy.wait_send()
    assert len(copies.all) <= N_SEM, len(copies.all)


def per_device(inputs, norm_gain, w_up, w_down, grad_out):
    vmem = pl.BlockSpec(memory_space=pltpu.VMEM)
    hbm = pl.BlockSpec(memory_space=pl.ANY)
    scratch = [
        ((D, F), BF16), ((F, D), BF16),
        ((16, R, D), BF16), ((16, R, D), BF16),
        ((T, D), BF16), ((T, D), BF16),
        ((H, 2 * T), BF16), ((H, T), BF16), ((2 * T, H), BF16),
        ((T, F), F32), ((T, F), F32),
        ((2 * T, F), BF16), ((T, F), BF16), ((F, 2 * T), BF16),
        ((4, 4, R, D), BF16), ((4, 4, R, D), BF16),
        ((2, 3, 4, R, H), BF16), ((2, 3, 4, R, H), BF16),
        ((3, R, D), BF16), ((3, R, D), BF16),
        ((4, 2, 160, F), BF16), ((2, 3, 160, F), BF16), ((2, 160, F), BF16),
        ((4, 2, 80, H), BF16), ((2, 3, 80, H), BF16), ((2, 80, H), BF16),
        ((4, 8, 128), F32), ((4, 8, 128), F32),
        ((4, 20, 128), F32), ((4, 20, 128), F32), ((4, 20, 128), F32),
        ((2, 20, 128), F32), ((2, 20, 128), F32),
        ((R, D), F32),
    ]
    out, gin, gup, gdn, gg = pl.pallas_call(
        kernel,
        out_shape=(
            jax.ShapeDtypeStruct((R, D), BF16),
            jax.ShapeDtypeStruct((R, D), BF16),
            jax.ShapeDtypeStruct((D, F), BF16),
            jax.ShapeDtypeStruct((F, D), BF16),
            jax.ShapeDtypeStruct((D // 128, 128), F32),
        ),
        in_specs=[vmem, vmem, hbm, hbm, vmem],
        out_specs=(vmem,) * 5,
        scratch_shapes=[pltpu.VMEM(s, t) for s, t in scratch]
        + [
            pltpu.SemaphoreType.DMA((N_SEM,)),
            pltpu.SemaphoreType.DMA((N_SEM,)),
            pltpu.SemaphoreType.DMA((2,)),
        ],
        compiler_params=pltpu.CompilerParams(
            collective_id=0, has_side_effects=True, vmem_limit_bytes=62 << 20
        ),
    )(inputs, norm_gain.reshape(1, D), w_up, w_down, grad_out)
    return out, gin, gup, gdn, gg.reshape(D)


def solution(mesh):
    return jax.shard_map(
        per_device,
        mesh=mesh,
        in_specs=(
            P(("dp", "tensor"), None),
            P(),
            P(None, "tensor"),
            P("tensor", None),
            P(("dp", "tensor"), None),
        ),
        out_specs=(
            P(("dp", "tensor"), None),
            P(("dp", "tensor"), None),
            P(None, "tensor"),
            P("tensor", None),
            P(),
        ),
        check_vma=False,
    )
```

time: 602 us -> 192 us (0.32)
  waiting for transfers between devices: 393 us -> 0 us
  Pallas kernels: 0 us -> 178 us
  blocking collectives: 123 us -> 0 us
  matrix products: 26.8 us -> 0 us
  other arithmetic: 15.9 us -> 0 us
  between operations: 14.5 us -> 0.64 us
  local copies, waits for them, and re-layouts: 20.8 us -> 10.8 us
    psum x1 -> x0, waiting for transfers between devices: 217 us -> none  [per_device(): lax.psum(up_part.astype(jnp.bfloat16), 'dp').astype(jnp.float32)]
    pallas_call x0 -> x1, Pallas kernels: none -> 178 us  [per_device(): pl.pallas_call(kernel, out_shape=(jax.ShapeDtypeStruct((R, D), BF16), jax...]
    all_gather x2 -> x0, waiting for transfers between devices: 154 us -> none  [the longest x1 78.2 us: per_device(): cotangent = lax.all_gather(grad_out, 'tensor', axis=0, tiled=True)]
    psum x1 -> x0, blocking collectives: 85.9 us -> none  [per_device(): lax.psum(jnp.sum(grad_xq * widened * inverse, axis=0), ('dp', 'tensor'))]
    pmax x1 -> x0, blocking collectives: 37.6 us -> none  [per_device(): peak_value = lax.pmax(jnp.max(hidden), 'tensor') + 1e-06]
    dot_general x6 -> x0, matrix products: 26.8 us -> none  [the longest x1 5.58 us: per_device(): lax.dot_general(gathered, grad_z, CONTRACT_ROWS, preferred_element_type=j...]
    reduce_scatter x2 -> x0, waiting for transfers between devices: 20.6 us -> none  [the longest x1 20.6 us: per_device(): lax.psum_scatter(lax.dot_general(picked, w_up, CONTRACT_COLS, preferred_e...]
    convert_element_type x3 -> x0, other arithmetic: 8.75 us -> none  [the longest x1 4.56 us: per_device(): hidden_q = (h_scale * staircase(hidden / h_scale)).astype(jnp.bfloat16)]
  transfers between devices with their start and end apart: 5 -> 0, of which waited for: 4 -> 0; matrix products, arithmetic and copies ran while one was open for 6% -> 0% of each run, Pallas kernels for 0% -> 0%
where the time goes in v1:
time: 192 us; the launch traced here: 189 us
  Pallas kernels  178 us (93%)
  local copies, waits for them, and re-layouts  10.8 us (6%)
    pallas_call x1, Pallas kernels, per_device(): pl.pallas_call(kernel, out_shape=(jax.ShapeDtypeStruct((R, D), BF16), jax...  178 us
    unnamed x9, local copies, waits for them, and re-layouts  9.49 us

profile of v1, /device:TPU:1, one launch (start us, length us, event | category | flops | bytes accessed | tf_op | source)
XLA Modules:
  0.0 189.2 jit_solution(13640607189739762943)
XLA Ops:
  0.6 1.3 reshape.16.gain_ref
  1.9 177.8 %shard_map.92 = (bf16[24,2560]{1,0:T(8,128)(2,1)}, bf16[24,2560]{1,0:T(8,128)(2,1)}, bf16[2560,640]{1,0:T(8,128)(2,1)}, bf16[640,2560]{1,0:T(8,128)(2,1)}, f32[20,128]{1,0:T(8,128)}) custom-call(bf16[24,2560]{1,0:T(8,128)(2,1)} %x_ref.1, f32[1,2560]{1,0:T(1,128)} %reshape.16.gain_ref, bf16[2560,640]{1,0:T(8,128)(2,1)} %wu_hbm.1, bf16[640,2560]{1,0:T(8,128)(2,1)} %wd_hbm.1, ...), custom_call_target="tpu_custom_call" | custom-call | tf_op jit(solution)/shard_map/pallas_call | solution.py:542
  179.7 1.6 copy.15
  181.3 1.6 copy.16
  182.9 0.0 copy-start
  182.9 4.1 %copy.17 = bf16[2560,640]{1,0:T(8,128)(2,1)} copy(bf16[2560,640]{1,0:T(8,128)(2,1)} %get-tuple-element.22) | data formatting | bytes 6553600
  186.9 0.0 copy-done
  186.9 0.0 copy-start.1
  186.9 1.7 copy.18
  188.6 0.0 copy-done.1
  188.6 0.6 copy.19
Async XLA Ops:
  182.9 4.1 %copy-start = (bf16[640,2560]{1,0:T(8,128)(2,1)S(1)}, bf16[640,2560]{1,0:T(8,128)(2,1)}, u32[]{:S(2)}) copy-start(bf16[640,2560]{1,0:T(8,128)(2,1)} %get-tuple-element.23) | copy-start | bytes 9830404
  186.9 1.7 copy-start.1

commit v2 on v1

--- a/solution.py
+++ b/solution.py
@@ -81,7 +81,7 @@
     x_ref, gain_ref, wu_hbm, wd_hbm, go_ref,
     out_ref, gin_ref, gup_ref, gdn_ref, gg_ref,
     wu, wd, cg, qg, c2, q2, aa, ss, cc, ghq, pa, gz2, hq, ht,
-    po, px, ro, rx, zo, zx, u, ur, uz, d, dr, dz,
+    po, px, ro, rx, zo, zx, w, wr, wz,
     py, pz, gy, gzl, gx, gc, gh, gfull, send, recv, local,
 ):
     dp, tn = lax.axis_index("dp"), lax.axis_index("tensor")
@@ -146,7 +146,7 @@
     inverse = lax.rsqrt(jnp.mean(wide * wide, axis=1, keepdims=True) + 1e-05)
     for i in range(D // 128):
         cols = slice(i * 128, (i + 1) * 128)
-        normed = wide[:, cols] * inverse * gain_ref[:, cols]
+        normed = wide[:, cols] * inverse * gain_ref[i : i + 1, :]
         q = quantize(normed, jnp.abs(normed), 1.5)
         qg[block(y, zl), :, cols] = q.astype(BF16)
 
@@ -250,9 +250,9 @@
     pyx = [go(py.at[y], py.at[y], peer) for peer in y_peers]
 
     class Ring:
-        def __init__(self, pos, plus, minus, view, got, add):
+        def __init__(self, pos, plus, minus, view, got, tiles, cut):
             self.pos, self.to = pos, (plus, minus)
-            self.view, self.got, self.add = view, got, add
+            self.view, self.got, self.tiles, self.cut = view, got, tiles, cut
             self.last = [None, None]
 
         def send(self, s, way):
@@ -264,184 +264,33 @@
             for way in (0, 1):
                 self.last[way].wait_recv()
                 j = mod(self.pos - 2 - s) if way == 0 else mod(self.pos + 2 + s)
-                self.add(j, way, s)
+                mine, theirs = self.view(j, way), self.got.at[way, s]
+
+                @pl.loop(0, self.tiles)
+                def _(i):
+                    at = self.cut(i)
+                    both = mine[at].astype(F32) + theirs[at].astype(F32)
+                    mine[at] = both.astype(BF16)
+
                 if s < 2:
                     self.send(s + 1, way)
 
-    def adder(view, got, tiles, cut):
-        def add(j, way, s):
-            mine, theirs = view(j, way), got.at[way, s]
-
-            @pl.loop(0, tiles)
-            def _(i):
-                at = cut(i)
-                mine[at] = (mine[at].astype(F32) + theirs[at].astype(F32)).astype(BF16)
-
-        return add
-
-    def rows_of(n):
-        return lambda i: (pl.ds(pl.multiple_of(i * n, n), n), slice(None))
-
-    def u_view(j, way):
-        return u.at[j, way]
-
-    def d_view(j, way):
-        return d.at[j, way]
-
-    def p_view(buf):
-        return lambda j, way: buf.at[j, :, :, pl.ds(way * H, H)]
-
-    up = Ring(x, xp, xm, u_view, ur, adder(u_view, ur, 5, rows_of(32)))
-    down = Ring(x, xp, xm, d_view, dr, adder(d_view, dr, 5, rows_of(16)))
-    out = Ring(y, yp, ym, p_view(po), ro, adder(p_view(po), ro, 4, lambda i: i))
-    gin = Ring(y, yp, ym, p_view(px), rx, adder(p_view(px), rx, 4, lambda i: i))
-
-    aax.wait_recv()
-    gzx.wait_recv()
-
-    def up_chunk(j):
-        rows = pl.ds(pl.multiple_of(j * 320, 320), 320)
-        u[j] = dot(aa[rows, :], gz2[...]).reshape(2, 160, F).astype(BF16)
-
-    up_chunk(mod(x - 1))
-    up.send(0, 0)
-    up_chunk(mod(x + 1))
-    up.send(0, 1)
-    up_chunk(mod(x + 2))
-    up_chunk(x)
-
-    for copy in pyx:
-        copy.wait_recv()
-    peak = jnp.maximum(jnp.maximum(py[0], py[1]), jnp.maximum(py[2], py[3]))
-    pz[zl] = peak
-    pzx = [go(pz.at[zl], pz.at[zl], peer) for peer in z_peers]
-
-    @pl.loop(0, 5)
-    def _(i):
-        ns = pl.ds(pl.multiple_of(i * 512, 512), 512)
-        part = dot(gz2[pl.ds(0, T), :], wu[ns, :], NT)
-        px[:, :, :, ns] = part.reshape(4, 4, R, 512).astype(BF16)
-
-    gin.send(0, 0)
-    gin.send(0, 1)
-
-    for copy in pzx:
-        copy.wait_recv()
-    peak = jnp.maximum(jnp.maximum(pz[0], pz[1]), jnp.maximum(pz[2], pz[3]))
-    floor = (peak[0:1, :] + 1e-06) * 0.125
-
-    @pl.loop(0, T // 128)
-    def _(i):
-        rows = pl.ds(pl.multiple_of(i * 128, 128), 128)
-        for j in range(F // 128):
-            cols = slice(j * 128, (j + 1) * 128)
-            active = pa[rows, cols]
-            hidden = active * active
-            q = quantize(hidden, hidden, floor)
-            hq[rows, cols] = q.astype(BF16)
-            ht[cols, rows] = q.T.astype(BF16)
-
-    htx = go(ht.at[:, pl.ds(0, T)], ht.at[:, pl.ds(T, T)], other)
-    up.take(0)
-
-    @pl.loop(0, 5)
-    def _(i):
-        ns = pl.ds(pl.multiple_of(i * 512, 512), 512)
-        part = dot(hq[...], wd[:, ns])
-        po[:, :, :, ns] = part.reshape(4, 4, R, 512).astype(BF16)
-
-    ccx.wait_recv()
-    htx.wait_recv()
-
-    def down_chunk(j):
-        rows = pl.ds(pl.multiple_of(j * 160, 160), 160)
-        d[j] = dot(ht[rows, :], cc[...]).reshape(2, 80, H).astype(BF16)
-
-    down_chunk(mod(x - 1))
-    down.send(0, 0)
-    down_chunk(mod(x + 1))
-    down.send(0, 1)
-    out.send(0, 0)
-    out.send(0, 1)
-    down_chunk(mod(x + 2))
-    down_chunk(x)
-
-    gin.take(0)
-    up.take(1)
-    down.take(0)
-    out.take(0)
-    up.take(2)
-    uzx = go(u.at[x], uz, zfar)
-    gin.take(1)
-    down.take(1)
-    out.take(1)
-    gin.take(2)
-
-    def scatter_z(buf, got):
-        return [
-            go(buf.at[y, mod(zl + k)], got.at[k - 1], z_peers[k - 1]) for k in (1, 2, 3)
-        ]
-
-    gin_z = scatter_z(px, zx)
-    down.take(2)
-    dzx = go(d.at[x], dz, zfar)
-    out.take(2)
-    out_z = scatter_z(po, zo)
-
-    for copy in gin_z:
-        copy.wait_recv()
-
-    def total(buf, got, cols):
-        t = buf[y, zl, :, cols].astype(F32) + got[0, :, cols].astype(F32)
-        return t + got[1, :, cols].astype(F32) + got[2, :, cols].astype(F32)
-
-    dots = jnp.zeros((R, 128), F32)
-    for i in range(D // 128):
-        cols = slice(i * 128, (i + 1) * 128)
-        g = total(px, zx, cols)
-        w = x_ref[:, cols].astype(F32)
-        gfull[:, cols] = g
-        dots = dots + g * gain_ref[:, cols] * w
-        gy[y, i : i + 1, :] = jnp.sum(g * w * inverse, axis=0, keepdims=True)
-    gyx = [go(gy.at[y], gy.at[y], peer) for peer in y_peers]
-    mean = jnp.sum(dots, axis=1, keepdims=True) * (1.0 / D)
-    cubed = inverse * inverse * inverse * mean
-    for i in range(D // 128):
-        cols = slice(i * 128, (i + 1) * 128)
-        w = x_ref[:, cols].astype(F32)
-        gin_ref[:, cols] = (
-            inverse * (gfull[:, cols] * gain_ref[:, cols]) - w * cubed
-        ).astype(BF16)
-
-    for copy in gyx:
-        copy.wait_recv()
-    gzl[zl] = gy[0] + gy[1] + gy[2] + gy[3]
-    gzx2 = [go(gzl.at[zl], gzl.at[zl], peer) for peer in z_peers]
-
-    def spread(own, chunk, buf, at_chunk, at_half):
-        res = []
-        at = buf.at[at_chunk(c, x)]
-        res.append((go(at, at, xp), go(at, at, xm)))
-        res.append(go(at, at, other))
-        return res
-
-    def up_rows(cc_, j, way=None):
-        if way is None:
-            return (pl.ds(pl.multiple_of(cc_ * H + j * 320, 320), 320), slice(None))
-        start = cc_ * H + j * 320 + way * 160
-        return (pl.ds(pl.multiple_of(start, 160), 160), slice(None))
-
-    def down_rows(cc_, j, way=None):
-        cols = pl.ds(pl.multiple_of(cc_ * H, H), H)
-        if way is None:
-            return (pl.ds(pl.multiple_of(j * 160, 160), 160), cols)
-        return (pl.ds(pl.multiple_of(j * 160 + way * 80, 80), 80), cols)
-
-    class Spread:
-        def __init__(self, buf, where):
-            self.buf, self.where = buf, where
+    class Part:
+        def __init__(self, n, buf, where):
+            self.n, self.buf, self.where = n, buf, where
+            self.ring = Ring(
+                x, xp, xm, lambda j, way: w.at[n, j, way], wr.at[n], 5,
+                lambda i: pl.ds(pl.multiple_of(i * 16, 16), 16),
+            )
+
+        def cross_z(self):
+            self.far = go(w.at[self.n, x], wz.at[self.n], zfar)
 
         def begin(self):
+            self.far.wait_recv()
+            for way in (0, 1):
+                both = w[self.n, x, way].astype(F32) + wz[self.n, way].astype(F32)
+                self.buf[self.where(c, x, way)] = both.astype(BF16)
             at = self.buf.at[self.where(c, x)]
             self.plus, self.minus = go(at, at, xp), go(at, at, xm)
             self.cross = [go(at, at, other)]
@@ -470,18 +319,193 @@
             for copy in self.cross:
                 copy.wait_recv()
 
-    uzx.wait_recv()
-    for way in (0, 1):
-        gup_ref[up_rows(c, x, way)] = (
-            u[x, way].astype(F32) + uz[way].astype(F32)
+    def up_rows(p):
+        def where(core, j, way=None):
+            start = core * H + j * 320 + p * 160 + (0 if way is None else way * 80)
+            n = 160 if way is None else 80
+            return (pl.ds(pl.multiple_of(start, n), n), slice(None))
+
+        return where
+
+    def down_rows(p):
+        def where(core, j, way=None):
+            cols = pl.ds(pl.multiple_of(core * H + p * F, 128), F)
+            start = j * 160 + (0 if way is None else way * 80)
+            n = 160 if way is None else 80
+            return (pl.ds(pl.multiple_of(start, n), n), cols)
+
+        return where
+
+    j1, j2 = Part(0, gup_ref, up_rows(0)), Part(1, gup_ref, up_rows(1))
+    j3, j4 = Part(2, gdn_ref, down_rows(0)), Part(3, gdn_ref, down_rows(1))
+
+    def p_view(buf):
+        return lambda j, way: buf.at[j, :, :, pl.ds(way * H, H)]
+
+    out = Ring(y, yp, ym, p_view(po), ro, 4, lambda i: i)
+    gin = Ring(y, yp, ym, p_view(px), rx, 4, lambda i: i)
+
+    aax.wait_recv()
+    gzx.wait_recv()
+
+    def up_chunk(p, j):
+        rows = pl.ds(pl.multiple_of(j * 320 + p * 160, 160), 160)
+        w[p, j] = dot(aa[rows, :], gz2[...]).reshape(2, 80, F).astype(BF16)
+
+    for p, part in ((0, j1), (1, j2)):
+        up_chunk(p, mod(x - 1))
+        part.ring.send(0, 0)
+        up_chunk(p, mod(x + 1))
+        part.ring.send(0, 1)
+    up_chunk(0, mod(x + 2))
+    up_chunk(1, mod(x + 2))
+
+    for copy in pyx:
+        copy.wait_recv()
+    peak = jnp.maximum(jnp.maximum(py[0], py[1]), jnp.maximum(py[2], py[3]))
+    pz[zl] = peak
+    pzx = [go(pz.at[zl], pz.at[zl], peer) for peer in z_peers]
+
+    up_chunk(0, x)
+    up_chunk(1, x)
+
+    @pl.loop(0, 5)
+    def _(i):
+        ns = pl.ds(pl.multiple_of(i * 512, 512), 512)
+        part = dot(gz2[pl.ds(0, T), :], wu[ns, :], NT)
+        px[:, :, :, ns] = part.reshape(4, 4, R, 512).astype(BF16)
+
+    j1.ring.take(0)
+    gin.send(0, 0)
+    gin.send(0, 1)
+    j2.ring.take(0)
+
+    for copy in pzx:
+        copy.wait_recv()
+    peak = jnp.maximum(jnp.maximum(pz[0], pz[1]), jnp.maximum(pz[2], pz[3]))
+    floor = (peak[0:1, :] + 1e-06) * 0.125
+
+    @pl.loop(0, T // 128)
+    def _(i):
+        rows = pl.ds(pl.multiple_of(i * 128, 128), 128)
+        for j in range(F // 128):
+            cols = slice(j * 128, (j + 1) * 128)
+            active = pa[rows, cols]
+            hidden = active * active
+            q = quantize(hidden, hidden, floor)
+            hq[rows, cols] = q.astype(BF16)
+            ht[cols, rows] = q.T.astype(BF16)
+
+    htx = go(ht.at[:, pl.ds(0, T)], ht.at[:, pl.ds(T, T)], other)
+    j1.ring.take(1)
+    j2.ring.take(1)
+    gin.take(0)
+
+    ccx.wait_recv()
+    htx.wait_recv()
+
+    def down_chunk(j):
+        rows = pl.ds(pl.multiple_of(j * 160, 160), 160)
+        for p in (0, 1):
+            part = dot(ht[rows, :], cc[:, p * F : (p + 1) * F])
+            w[2 + p, j] = part.reshape(2, 80, F).astype(BF16)
+
+    down_chunk(mod(x - 1))
+    j3.ring.send(0, 0)
+    down_chunk(mod(x + 1))
+    j3.ring.send(0, 1)
+    j1.ring.take(2)
+    j1.cross_z()
+    j4.ring.send(0, 0)
+    j4.ring.send(0, 1)
+    down_chunk(mod(x + 2))
+    j2.ring.take(2)
+    j2.cross_z()
+    down_chunk(x)
+
+    @pl.loop(0, 5)
+    def _(i):
+        ns = pl.ds(pl.multiple_of(i * 512, 512), 512)
+        part = dot(hq[...], wd[:, ns])
+        po[:, :, :, ns] = part.reshape(4, 4, R, 512).astype(BF16)
+
+    j3.ring.take(0)
+    gin.take(1)
+    out.send(0, 0)
+    out.send(0, 1)
+    j4.ring.take(0)
+
+    def scatter_z(buf, got):
+        return [
+            go(buf.at[y, mod(zl + k)], got.at[k - 1], z_peers[k - 1]) for k in (1, 2, 3)
+        ]
+
+    j3.ring.take(1)
+    gin.take(2)
+    gin_z = scatter_z(px, zx)
+    j4.ring.take(1)
+    j1.begin()
+    j3.ring.take(2)
+    j3.cross_z()
+    out.take(0)
+    j4.ring.take(2)
+    j4.cross_z()
+    j1.middle()
+    out.take(1)
+    j2.begin()
+    j1.end()
+    j2.middle()
+
+    for copy in gin_z:
+        copy.wait_recv()
+
+    def total(buf, got, cols):
+        t = buf[y, zl, :, cols].astype(F32) + got[0, :, cols].astype(F32)
+        return t + got[1, :, cols].astype(F32) + got[2, :, cols].astype(F32)
+
+    dots = jnp.zeros((R, 128), F32)
+    for i in range(D // 128):
+        cols = slice(i * 128, (i + 1) * 128)
+        g = total(px, zx, cols)
+        t = x_ref[:, cols].astype(F32)
+        gfull[:, cols] = g
+        dots = dots + g * gain_ref[i : i + 1, :] * t
+        gy[y, i : i + 1, :] = jnp.sum(g * t * inverse, axis=0, keepdims=True)
+    gyx = [go(gy.at[y], gy.at[y], peer) for peer in y_peers]
+    out.take(2)
+    out_z = scatter_z(po, zo)
+    mean = jnp.sum(dots, axis=1, keepdims=True) * (1.0 / D)
+    cubed = inverse * inverse * inverse * mean
+    for i in range(D // 128):
+        cols = slice(i * 128, (i + 1) * 128)
+        t = x_ref[:, cols].astype(F32)
+        gin_ref[:, cols] = (
+            inverse * (gfull[:, cols] * gain_ref[i : i + 1, :]) - t * cubed
         ).astype(BF16)
-    spread_up = Spread(gup_ref, up_rows)
-    spread_up.begin()
+
+    for copy in gyx:
+        copy.wait_recv()
+    gzl[zl] = gy[0] + gy[1] + gy[2] + gy[3]
+    gzx2 = [go(gzl.at[zl], gzl.at[zl], peer) for peer in z_peers]
+    j2.end()
+    j3.begin()
 
     for copy in gzx2:
         copy.wait_recv()
     gx[x] = gzl[0] + gzl[1] + gzl[2] + gzl[3]
     gxx = [go(gx.at[x], gx.at[x], peer) for peer in x_peers]
+    j3.middle()
+    j4.begin()
+
+    for copy in gxx:
+        copy.wait_recv()
+    gc[c] = gx[0] + gx[1] + gx[2] + gx[3]
+    gcx = go(gc.at[c], gc.at[c], other)
+    j3.end()
+    j4.middle()
+    gcx.wait_recv()
+    gh[zh] = gc[0] + gc[1]
+    ghx = go(gh.at[zh], gh.at[zh], zfar)
 
     for copy in out_z:
         copy.wait_recv()
@@ -489,31 +513,11 @@
         cols = slice(i * 128, (i + 1) * 128)
         out_ref[:, cols] = total(po, zo, cols).astype(BF16)
 
-    spread_up.middle()
-
-    for copy in gxx:
-        copy.wait_recv()
-    gc[c] = gx[0] + gx[1] + gx[2] + gx[3]
-    gcx = go(gc.at[c], gc.at[c], other)
-
-    dzx.wait_recv()
-    for way in (0, 1):
-        gdn_ref[down_rows(c, x, way)] = (
-            d[x, way].astype(F32) + dz[way].astype(F32)
-        ).astype(BF16)
-    spread_down = Spread(gdn_ref, down_rows)
-    spread_down.begin()
-
-    gcx.wait_recv()
-    gh[zh] = gc[0] + gc[1]
-    ghx = go(gh.at[zh], gh.at[zh], zfar)
-    spread_up.end()
+    j4.end()
     ghx.wait_recv()
     gg_ref[...] = gh[0] + gh[1]
-    spread_down.middle()
-    spread_down.end()
-    spread_up.finish()
-    spread_down.finish()
+    for part in (j1, j2, j3, j4):
+        part.finish()
     for copy in copies.all:
         copy.wait_send()
     assert len(copies.all) <= N_SEM, len(copies.all)
@@ -532,8 +536,7 @@
         ((4, 4, R, D), BF16), ((4, 4, R, D), BF16),
         ((2, 3, 4, R, H), BF16), ((2, 3, 4, R, H), BF16),
         ((3, R, D), BF16), ((3, R, D), BF16),
-        ((4, 2, 160, F), BF16), ((2, 3, 160, F), BF16), ((2, 160, F), BF16),
-        ((4, 2, 80, H), BF16), ((2, 3, 80, H), BF16), ((2, 80, H), BF16),
+        ((4, 4, 2, 80, F), BF16), ((4, 2, 3, 80, F), BF16), ((4, 2, 80, F), BF16),
         ((4, 8, 128), F32), ((4, 8, 128), F32),
         ((4, 20, 128), F32), ((4, 20, 128), F32), ((4, 20, 128), F32),
         ((2, 20, 128), F32), ((2, 20, 128), F32),
@@ -542,11 +545,11 @@
     out, gin, gup, gdn, gg = pl.pallas_call(
         kernel,
         out_shape=(
-            jax.ShapeDtypeStruct((R, D), BF16),
-            jax.ShapeDtypeStruct((R, D), BF16),
-            jax.ShapeDtypeStruct((D, F), BF16),
-            jax.ShapeDtypeStruct((F, D), BF16),
-            jax.ShapeDtypeStruct((D // 128, 128), F32),
+            pltpu.VMEM((R, D), BF16),
+            pltpu.VMEM((R, D), BF16),
+            pltpu.VMEM((D, F), BF16),
+            pltpu.VMEM((F, D), BF16),
+            pltpu.VMEM((D // 128, 128), F32),
         ),
         in_specs=[vmem, vmem, hbm, hbm, vmem],
         out_specs=(vmem,) * 5,
@@ -557,9 +560,9 @@
             pltpu.SemaphoreType.DMA((2,)),
         ],
         compiler_params=pltpu.CompilerParams(
-            collective_id=0, has_side_effects=True, vmem_limit_bytes=62 << 20
+            collective_id=0, has_side_effects=True, vmem_limit_bytes=46 << 20
         ),
-    )(inputs, norm_gain.reshape(1, D), w_up, w_down, grad_out)
+    )(inputs, norm_gain.reshape(D // 128, 128), w_up, w_down, grad_out)
     return out, gin, gup, gdn, gg.reshape(D)
 
 

time: 192 us -> 164 us (0.85); the launches traced: 189 us -> 164 us
  Pallas kernels: 178 us -> 155 us
  local copies, waits for them, and re-layouts: 10.8 us -> 7.82 us
    pallas_call x1, Pallas kernels: 178 us -> 155 us  [per_device(): pl.pallas_call(kernel, out_shape=(pltpu.VMEM((R, D), BF16), pltpu.VMEM((R...]
    unnamed x9 -> x11, local copies, waits for them, and re-layouts: 9.49 us -> 7.82 us
where the time goes in v2:
time: 164 us
  Pallas kernels  155 us (95%)
  local copies, waits for them, and re-layouts  7.82 us (5%)
    pallas_call x1, Pallas kernels, per_device(): pl.pallas_call(kernel, out_shape=(pltpu.VMEM((R, D), BF16), pltpu.VMEM((R...  155 us
    unnamed x11, local copies, waits for them, and re-layouts  7.82 us

profile of v2, /device:TPU:1, one launch (start us, length us, event | category | flops | bytes accessed | tf_op | source)
XLA Modules:
  0.0 163.6 jit_solution(7683299534525416964)
XLA Ops:
  0.6 0.0 copy-start
  0.6 0.9 copy-done
  1.5 0.0 copy-start.1
  1.5 0.9 copy-done.1
  2.4 0.0 copy-start.2
  2.4 0.7 copy-done.2
  3.1 155.1 %shard_map.92 = (bf16[24,2560]{1,0:T(8,128)(2,1)S(1)}, bf16[24,2560]{1,0:T(8,128)(2,1)S(1)}, bf16[2560,640]{1,0:T(8,128)(2,1)S(1)}, bf16[640,2560]{1,0:T(8,128)(2,1)S(1)}, f32[20,128]{1,0:T(8,128)S(1)}) custom-call(bf16[24,2560]{1,0:T(8,128)(2,1)S(1)} %copy-done, f32[20,128]{1,0:T(8,128)S(1)} %bitcast.3, bf16[2560,640]{1,0:T(8,128)(2,1)} %wu_hbm.1, ...), custom_call_target="tpu_custom_call" | custom-call | tf_op jit(solution)/shard_map/pallas_call | solution.py:545
  158.2 0.7 copy.15
  158.9 0.6 copy.19
  159.5 0.6 copy.16
  160.1 1.7 %copy.17 = bf16[2560,640]{1,0:T(8,128)(2,1)} copy(bf16[2560,640]{1,0:T(8,128)(2,1)S(1)} %get-tuple-element.17) | data formatting | bytes 6553600
  161.9 1.7 %copy.18 = bf16[640,2560]{1,0:T(8,128)(2,1)} copy(bf16[640,2560]{1,0:T(8,128)(2,1)S(1)} %get-tuple-element.18) | data formatting | bytes 6553600
Async XLA Ops:
  0.6 0.9 copy-start
  1.5 0.9 copy-start.1
  2.4 0.7 copy-start.2

commit v3 on v2

v3 whole, which is shorter than its diff:
```python
import functools

import jax
import jax.numpy as jnp
from jax import lax
from jax.experimental import pallas as pl
from jax.experimental.pallas import tpu as pltpu
from jax.sharding import PartitionSpec as P

MESH = pl.DeviceIdType.MESH
F32 = jnp.float32
BF16 = jnp.bfloat16

D = 2560
F = 640
T = 384
R = 24
H = D // 2
N_SEND, N_RECV = 94, 143

SINE = (
    0.9999999958410793,
    -6.579735564529717,
    12.987846451008128,
    -12.207473944175224,
    6.687349899038311,
    -2.367236060103434,
    0.5102235956366108,
)
NT = (((1,), (1,)), ((), ()))
NN = (((1,), (0,)), ((), ()))


def dot(a, b, dims=NN):
    return lax.dot_general(a, b, dims, preferred_element_type=F32)


def staircase(values):
    r = values - jnp.floor(values + 0.5)
    s = r * r
    p = jnp.full_like(s, SINE[-1])
    for c in SINE[-2::-1]:
        p = p * s + c
    return values - p * r


def block_peak(values):
    lane = lax.broadcasted_iota(jnp.int32, values.shape, 1)
    for s in (1, 2, 4, 8):
        up = pltpu.roll(values, s, 1)
        down = pltpu.roll(values, 128 - s, 1)
        values = jnp.maximum(values, jnp.where((lane & s) != 0, up, down))
    return values


def quantize(values, magnitude, floor):
    peak = jnp.maximum(block_peak(magnitude), floor)
    return peak * (1.0 / 6.0) * staircase(values * (6.0 / peak))


class Copies:
    def __init__(self, send, recv):
        self.send, self.recv = send, recv
        self.count, self.spare, self.most, self.open = 0, [], 0, []

    def start(self, src, dst, device):
        if self.spare:
            n = self.spare.pop()
        else:
            n = self.most
            self.most += 1
        copy = pltpu.make_async_remote_copy(
            src_ref=src,
            dst_ref=dst,
            send_sem=self.send.at[n],
            recv_sem=self.recv.at[self.count],
            device_id=device,
            device_id_type=MESH,
        )
        copy.start()
        self.count += 1
        self.open.append((copy, n))
        return copy

    def sent(self, upto=None):
        done = self.open[:upto]
        for copy, n in done:
            copy.wait_send()
            self.spare.append(n)
        self.open = self.open[len(done) :]


def kernel(
    x_hbm, gain_hbm, wu_hbm, wd_hbm, go_hbm,
    out_ref, gin_ref, gup_ref, gdn_ref, gg_ref,
    x_ref, gain_ref, wu, wd, cg, qg, c2, aa, ss, cc, ghq, pa, gz2, hq, ht,
    po, px, ro, rx, zo, zx, w, wr, wz,
    py, pz, gy, gzl, gx, gc, gh, gfull, mx, send, recv, local,
):
    dp, tn = lax.axis_index("dp"), lax.axis_index("tensor")
    zh, x, c = dp // 8, (dp // 2) % 4, dp % 2
    zl, y = tn // 4, tn % 4

    def dev(zh=zh, x=x, c=c, zl=zl, y=y):
        return ((zh * 4 + x) * 2 + c, zl * 4 + y)

    def mod(v):
        return lax.rem(v + 8, 4)

    def place(rel):
        return (rel + 1) % 4

    def block(rel, zz):
        return place(rel) * 4 + zz

    yp, ym = dev(y=mod(y + 1)), dev(y=mod(y - 1))
    xp, xm = dev(x=mod(x + 1)), dev(x=mod(x - 1))
    other = dev(c=1 - c)
    zfar = dev(zh=1 - zh)
    y_peers = [dev(y=mod(y + k)) for k in (1, 2, 3)]
    z_peers = [dev(zl=mod(zl + k)) for k in (1, 2, 3)]
    x_peers = [dev(x=mod(x + k)) for k in (1, 2, 3)]
    copies = Copies(send, recv)
    go = copies.start

    def load(src, dst, n):
        copy = pltpu.make_async_copy(src, dst, local.at[n])
        copy.start()
        return copy

    load_x = load(x_hbm, x_ref, 2)
    load_gain = load(gain_hbm, gain_ref, 3)
    load_own = load(go_hbm, cg.at[block(0, zl)], 4)
    load_up = load(wu_hbm, wu, 0)
    load_down = load(wd_hbm, wd, 1)

    barrier = pltpu.get_barrier_semaphore()
    peers = y_peers + z_peers + x_peers + [other, zfar]
    for peer in peers:
        pl.semaphore_signal(barrier, inc=1, device_id=peer, device_id_type=MESH)
    load_x.wait()
    wide = x_ref[...].astype(F32)
    inverse = lax.rsqrt(jnp.mean(wide * wide, axis=1, keepdims=True) + 1e-05)
    load_gain.wait()
    pl.semaphore_wait(barrier, len(peers))

    def gather_z(buf, src, k):
        return go(src, buf.at[block(0, zl)], z_peers[k - 1])

    def gather_y(buf, k, src=None):
        zz = mod(zl - k)
        src = buf.at[block(0, zz)] if src is None else src
        return go(src, buf.at[block(-1, zz)], yp), go(src, buf.at[block(1, zz)], ym)

    def forward(buf, k, pair):
        plus, minus = pair
        zz = mod(zl - k)
        left, right = (slice(None), pl.ds(0, H)), (slice(None), pl.ds(H, H))
        plus.wait_recv()
        a = go(buf.at[(block(-1, zz), *left)], buf.at[(block(2, zz), *left)], yp)
        minus.wait_recv()
        b = go(buf.at[(block(1, zz), *right)], buf.at[(block(2, zz), *right)], ym)
        return a, b

    cy, qy, cz, qz, cf, qf = {}, {}, {}, {}, [], []
    cy[0] = gather_y(cg, 0, go_hbm)
    cz[1] = gather_z(cg, go_hbm, 1)

    for i in range(D // 128):
        cols = slice(i * 128, (i + 1) * 128)
        normed = wide[:, cols] * inverse * gain_ref[i : i + 1, :]
        q = quantize(normed, jnp.abs(normed), 1.5)
        qg[block(0, zl), :, cols] = q.astype(BF16)

    mine = qg.at[block(0, zl)]
    qy[0] = gather_y(qg, 0)
    qz[1] = gather_z(qg, mine, 1)
    qz[3] = gather_z(qg, mine, 3)

    def next_q(k):
        qz[k].wait_recv()
        qy[k] = gather_y(qg, k)

    def next_c(k):
        cz[k].wait_recv()
        cy[k] = gather_y(cg, k)

    def forward_q(k):
        qf.extend(forward(qg, k, qy[k]))

    def forward_c(k):
        cf.extend(forward(cg, k, cy[k]))

    next_c(1)
    forward_c(0)
    forward_q(0)
    next_q(1)
    qz[2] = gather_z(qg, mine, 2)
    next_q(3)
    cz[3] = gather_z(cg, go_hbm, 3)
    forward_q(1)
    next_q(2)
    cz[2] = gather_z(cg, go_hbm, 2)
    forward_q(3)
    forward_c(1)
    next_c(3)
    forward_q(2)
    next_c(2)

    load_up.wait()
    near, last = (0, 12), (12, 4)

    def pre_group(group, most):
        b, n = group
        rows = slice(b * R, (b + n) * R)

        @pl.loop(0, 5)
        def _(i):
            ks = pl.ds(pl.multiple_of(i * 512, 512), 512)
            v = qg[b : b + n, :, ks].astype(F32).reshape(n * R, 512).astype(BF16)
            part = dot(v, wu[ks, :])

            @pl.when(i == 0)
            def _():
                pa[rows, :] = part

            @pl.when(i > 0)
            def _():
                pa[rows, :] += part

        @pl.loop(0, n)
        def _(i):
            at = pl.ds(pl.multiple_of(b * R + i * R, R), R)
            top = jnp.zeros((R, 128), F32)
            for j in range(F // 128):
                cols = slice(j * 128, (j + 1) * 128)
                active = jnp.maximum(pa[at, cols], 0.0)
                pa[at, cols] = active
                top = jnp.maximum(top, active)
            most[...] = jnp.maximum(most[...], top)

    mx[...] = jnp.zeros((R, 128), F32)
    pre_group(near, mx)
    for copy in qf:
        copy.wait_recv()
    forward_c(3)
    pre_group(last, mx)
    most = jnp.max(jnp.max(mx[...], axis=0, keepdims=True), axis=1, keepdims=True)
    py[y] = jnp.broadcast_to(most * most, (8, 128))
    pyx = [go(py.at[y], py.at[y], peer) for peer in y_peers]
    forward_c(2)

    def lay(i, start, put):
        cols = pl.ds(pl.multiple_of(start + i * 256, 256), 256)
        v = qg[:, :, cols].astype(F32).reshape(T, 256)
        put(pl.ds(pl.multiple_of(i * 256, 256), 256), v.T.astype(BF16))

    def put_other(rows, v):
        ss[rows, :] = v

    def put_own(rows, v):
        aa[rows, pl.ds(0, T)] = v

    @pl.loop(0, 5)
    def _(i):
        lay(i, (1 - c) * H, put_other)

    aax = go(ss, aa.at[:, pl.ds(T, T)], other)

    load_down.wait()
    other_half = pl.ds(pl.multiple_of((1 - c) * H, H), H)
    own_half = pl.ds(pl.multiple_of(c * H, H), H)
    gzx, ccx = [], []

    def grad_group(group):
        b, n = group
        rows = slice(b * R, (b + n) * R)

        @pl.loop(0, 5)
        def _(i):
            ks = pl.ds(pl.multiple_of(i * 512, 512), 512)
            v = cg[b : b + n, :, ks].astype(F32).reshape(n * R, 512).astype(BF16)
            c2[rows, ks] = v
            part = dot(v, wd[:, ks], NT)

            @pl.when(i == 0)
            def _():
                ghq[rows, :] = part

            @pl.when(i > 0)
            def _():
                ghq[rows, :] += part

        @pl.loop(0, n // 2)
        def _(i):
            at = pl.ds(pl.multiple_of(b * R + i * 2 * R, 2 * R), 2 * R)
            for j in range(F // 128):
                cols = slice(j * 128, (j + 1) * 128)
                gz2[at, cols] = (ghq[at, cols] * 2.0 * pa[at, cols]).astype(BF16)

        far = slice(T + b * R, T + (b + n) * R)
        gzx.append(go(gz2.at[rows], gz2.at[far], other))
        ccx.append(go(c2.at[rows, other_half], cc.at[far], other))

    load_own.wait()
    grad_group(near)

    @pl.loop(0, 5)
    def _(i):
        lay(i, c * H, put_own)

    for copy in pyx:
        copy.wait_recv()
    peak = jnp.maximum(jnp.maximum(py[0], py[1]), jnp.maximum(py[2], py[3]))
    pz[zl] = peak
    pzx = [go(pz.at[zl], pz.at[zl], peer) for peer in z_peers]
    for copy in cf:
        copy.wait_recv()
    grad_group(last)

    class Ring:
        def __init__(self, plus, minus, view, got, tiles, cut):
            self.to = (plus, minus)
            self.view, self.got, self.tiles, self.cut = view, got, tiles, cut
            self.last = [None, None]

        def send(self, s, way):
            at = self.view(-1 - s if way == 0 else 1 + s, way)
            self.last[way] = go(at, self.got.at[way, s], self.to[way])

        def take(self, s):
            for way in (0, 1):
                self.last[way].wait_recv()
                mine = self.view(-2 - s if way == 0 else 2 + s, way)
                theirs = self.got.at[way, s]

                @pl.loop(0, self.tiles)
                def _(i):
                    at = self.cut(i)
                    both = mine[at].astype(F32) + theirs[at].astype(F32)
                    mine[at] = both.astype(BF16)

                if s < 2:
                    self.send(s + 1, way)

    class Part:
        def __init__(self, n, buf, where):
            self.n, self.buf, self.where = n, buf, where
            self.ring = Ring(
                xp, xm, lambda rel, way: w.at[n, mod(x + rel), way], wr.at[n], 5,
                lambda i: pl.ds(pl.multiple_of(i * 16, 16), 16),
            )

        def cross_z(self):
            self.far = go(w.at[self.n, x], wz.at[self.n], zfar)

        def begin(self):
            self.far.wait_recv()
            for way in (0, 1):
                both = w[self.n, x, way].astype(F32) + wz[self.n, way].astype(F32)
                self.buf[self.where(c, x, way)] = both.astype(BF16)
            at = self.buf.at[self.where(c, x)]
            self.plus, self.minus = go(at, at, xp), go(at, at, xm)
            self.cross = [go(at, at, other)]

        def middle(self):
            self.plus.wait_recv()
            at = self.buf.at[self.where(c, mod(x - 1), 0)]
            self.fplus = go(at, at, xp)
            at = self.buf.at[self.where(c, mod(x - 1))]
            self.cross.append(go(at, at, other))
            self.minus.wait_recv()
            at = self.buf.at[self.where(c, mod(x + 1), 1)]
            self.fminus = go(at, at, xm)
            at = self.buf.at[self.where(c, mod(x + 1))]
            self.cross.append(go(at, at, other))

        def end(self):
            self.fplus.wait_recv()
            at = self.buf.at[self.where(c, mod(x + 2), 0)]
            self.cross.append(go(at, at, other))
            self.fminus.wait_recv()
            at = self.buf.at[self.where(c, mod(x + 2), 1)]
            self.cross.append(go(at, at, other))

        def finish(self):
            for copy in self.cross:
                copy.wait_recv()

    def up_rows(p):
        def where(core, j, way=None):
            start = core * H + j * 320 + p * 160 + (0 if way is None else way * 80)
            n = 160 if way is None else 80
            return (pl.ds(pl.multiple_of(start, n), n), slice(None))

        return where

    def down_rows(p):
        def where(core, j, way=None):
            cols = pl.ds(pl.multiple_of(core * H + p * F, 128), F)
            start = j * 160 + (0 if way is None else way * 80)
            n = 160 if way is None else 80
            return (pl.ds(pl.multiple_of(start, n), n), cols)

        return where

    j1, j2 = Part(0, gup_ref, up_rows(0)), Part(1, gup_ref, up_rows(1))
    j3, j4 = Part(2, gdn_ref, down_rows(0)), Part(3, gdn_ref, down_rows(1))

    def p_view(buf):
        return lambda rel, way: buf.at[place(rel), :, :, pl.ds(way * H, H)]

    out = Ring(yp, ym, p_view(po), ro, 4, lambda i: i)
    gin = Ring(yp, ym, p_view(px), rx, 4, lambda i: i)

    aax.wait_recv()
    for copy in gzx:
        copy.wait_recv()

    def up_chunk(p, j):
        rows = pl.ds(pl.multiple_of(j * 320 + p * 160, 160), 160)
        w[p, j] = dot(aa[rows, :], gz2[...]).reshape(2, 80, F).astype(BF16)

    mark = len(copies.open)
    up_chunk(0, mod(x - 1))
    j1.ring.send(0, 0)
    up_chunk(0, mod(x + 1))
    j1.ring.send(0, 1)
    up_chunk(0, mod(x + 2))

    @pl.loop(0, 5)
    def _(i):
        ns = pl.ds(pl.multiple_of(i * 512, 512), 512)
        part = dot(gz2[pl.ds(0, T), :], wu[ns, :], NT)
        px[:, :, :, ns] = part.reshape(4, 4, R, 512).astype(BF16)

    gin.send(0, 0)
    gin.send(0, 1)
    j1.ring.take(0)
    up_chunk(0, x)
    copies.sent(mark)

    for copy in pzx:
        copy.wait_recv()
    peak = jnp.maximum(jnp.maximum(pz[0], pz[1]), jnp.maximum(pz[2], pz[3]))
    floor = ((peak[0:1, :] + 1e-06) * 0.125).reshape(1, 1, 128)

    def hidden_tile(i):
        rows = slice(i * 128, (i + 1) * 128)

        @pl.loop(0, F // 128)
        def _(j):
            cols = pl.ds(pl.multiple_of(j * 128, 128), 128)
            active = pa[rows, cols]
            hidden = (active * active).T.reshape(8, 16, 128)
            most = jnp.maximum(jnp.max(hidden, axis=1, keepdims=True), floor)
            q = most * (1.0 / 6.0) * staircase(hidden * (6.0 / most))
            q = q.reshape(128, 128)
            ht[cols, rows] = q.astype(BF16)
            hq[rows, cols] = q.T.astype(BF16)

    hidden_tile(0)
    up_chunk(1, mod(x - 1))
    up_chunk(1, mod(x + 1))
    j1.ring.take(1)
    j2.ring.send(0, 0)
    j2.ring.send(0, 1)
    hidden_tile(1)
    up_chunk(1, mod(x + 2))
    up_chunk(1, x)
    hidden_tile(2)
    htx = go(ht.at[:, pl.ds(0, T)], ht.at[:, pl.ds(T, T)], other)
    gin.take(0)

    def down_chunk(j):
        rows = pl.ds(pl.multiple_of(j * 160, 160), 160)
        for p in (0, 1):
            part = dot(ht[rows, :], cc[:, p * F : (p + 1) * F])
            w[2 + p, j] = part.reshape(2, 80, F).astype(BF16)

    j1.ring.take(2)
    j1.cross_z()
    j2.ring.take(0)
    cc[pl.ds(0, T), :] = c2[:, own_half]
    for copy in ccx:
        copy.wait_recv()
    htx.wait_recv()
    down_chunk(mod(x - 1))
    j3.ring.send(0, 0)
    down_chunk(mod(x + 1))
    j3.ring.send(0, 1)
    j2.ring.take(1)
    gin.take(1)
    down_chunk(mod(x + 2))
    down_chunk(x)

    def out_tile(i):
        ns = slice(i * 512, (i + 1) * 512)
        part = dot(hq[...], wd[:, ns])
        po[:, :, :, ns] = part.reshape(4, 4, R, 512).astype(BF16)

    out_tile(0)
    j2.ring.take(2)
    j2.cross_z()
    j4.ring.send(0, 0)
    j4.ring.send(0, 1)
    out_tile(1)
    j3.ring.take(0)
    out_tile(2)
    out_tile(3)
    out_tile(4)
    out.send(0, 0)
    out.send(0, 1)

    def scatter_z(buf, got):
        return [
            go(buf.at[place(0), mod(zl + k)], got.at[k - 1], z_peers[k - 1]) for k in (1, 2, 3)
        ]

    gin.take(2)
    gin_z = scatter_z(px, zx)
    j3.ring.take(1)
    j4.ring.take(0)
    j1.begin()
    j3.ring.take(2)
    j3.cross_z()
    j4.ring.take(1)
    out.take(0)
    j4.ring.take(2)
    j4.cross_z()
    j1.middle()
    j2.begin()
    out.take(1)
    j1.end()
    j2.middle()
    out.take(2)
    out_z = scatter_z(po, zo)
    j2.end()

    for copy in gin_z:
        copy.wait_recv()

    def total(buf, got, cols):
        t = buf[place(0), zl, :, cols].astype(F32) + got[0, :, cols].astype(F32)
        return t + got[1, :, cols].astype(F32) + got[2, :, cols].astype(F32)

    dots = jnp.zeros((R, 128), F32)
    for i in range(D // 128):
        cols = slice(i * 128, (i + 1) * 128)
        g = total(px, zx, cols)
        t = x_ref[:, cols].astype(F32)
        gfull[:, cols] = g
        dots = dots + g * gain_ref[i : i + 1, :] * t
        gy[y, i : i + 1, :] = jnp.sum(g * t * inverse, axis=0, keepdims=True)
    gyx = [go(gy.at[y], gy.at[y], peer) for peer in y_peers]
    j3.begin()
    mean = jnp.sum(dots, axis=1, keepdims=True) * (1.0 / D)
    cubed = inverse * inverse * inverse * mean
    for i in range(D // 128):
        cols = slice(i * 128, (i + 1) * 128)
        t = x_ref[:, cols].astype(F32)
        gin_ref[:, cols] = (
            inverse * (gfull[:, cols] * gain_ref[i : i + 1, :]) - t * cubed
        ).astype(BF16)

    for copy in gyx:
        copy.wait_recv()
    gzl[zl] = gy[0] + gy[1] + gy[2] + gy[3]
    gzx2 = [go(gzl.at[zl], gzl.at[zl], peer) for peer in z_peers]
    j3.middle()
    j4.begin()
    for copy in gzx2:
        copy.wait_recv()
    gx[x] = gzl[0] + gzl[1] + gzl[2] + gzl[3]
    gxx = [go(gx.at[x], gx.at[x], peer) for peer in x_peers]
    j3.end()
    for copy in gxx:
        copy.wait_recv()
    gc[c] = gx[0] + gx[1] + gx[2] + gx[3]
    gcx = go(gc.at[c], gc.at[c], other)
    j4.middle()
    gcx.wait_recv()
    gh[zh] = gc[0] + gc[1]
    ghx = go(gh.at[zh], gh.at[zh], zfar)

    for copy in out_z:
        copy.wait_recv()
    for i in range(D // 128):
        cols = slice(i * 128, (i + 1) * 128)
        out_ref[:, cols] = total(po, zo, cols).astype(BF16)

    j4.end()
    ghx.wait_recv()
    gg_ref[...] = gh[0] + gh[1]
    for part in (j1, j2, j3, j4):
        part.finish()
    copies.sent()
    assert (copies.most, copies.count) == (N_SEND, N_RECV), (copies.most, copies.count)


def per_device(inputs, norm_gain, w_up, w_down, grad_out):
    vmem = pl.BlockSpec(memory_space=pltpu.VMEM)
    hbm = pl.BlockSpec(memory_space=pltpu.HBM)
    scratch = [
        ((R, D), BF16), ((D // 128, 128), F32),
        ((D, F), BF16), ((F, D), BF16),
        ((16, R, D), BF16), ((16, R, D), BF16),
        ((T, D), BF16),
        ((H, 2 * T), BF16), ((H, T), BF16), ((2 * T, H), BF16),
        ((T, F), F32), ((T, F), F32),
        ((2 * T, F), BF16), ((T, F), BF16), ((F, 2 * T), BF16),
        ((4, 4, R, D), BF16), ((4, 4, R, D), BF16),
        ((2, 3, 4, R, H), BF16), ((2, 3, 4, R, H), BF16),
        ((3, R, D), BF16), ((3, R, D), BF16),
        ((4, 4, 2, 80, F), BF16), ((4, 2, 3, 80, F), BF16), ((4, 2, 80, F), BF16),
        ((4, 8, 128), F32), ((4, 8, 128), F32),
        ((4, 20, 128), F32), ((4, 20, 128), F32), ((4, 20, 128), F32),
        ((2, 20, 128), F32), ((2, 20, 128), F32),
        ((R, D), F32), ((R, 128), F32),
    ]
    out, gin, gup, gdn, gg = pl.pallas_call(
        kernel,
        out_shape=(
            pltpu.VMEM((R, D), BF16),
            pltpu.VMEM((R, D), BF16),
            pltpu.VMEM((D, F), BF16),
            pltpu.VMEM((F, D), BF16),
            pltpu.VMEM((D // 128, 128), F32),
        ),
        in_specs=[hbm] * 5,
        out_specs=(vmem,) * 5,
        scratch_shapes=[pltpu.VMEM(s, t) for s, t in scratch]
        + [
            pltpu.SemaphoreType.DMA((N_SEND,)),
            pltpu.SemaphoreType.DMA((N_RECV,)),
            pltpu.SemaphoreType.DMA((5,)),
        ],
        compiler_params=pltpu.CompilerParams(
            collective_id=0, has_side_effects=True, vmem_limit_bytes=46 << 20
        ),
    )(inputs, norm_gain.reshape(D // 128, 128), w_up, w_down, grad_out)
    return out, gin, gup, gdn, gg.reshape(D)


def solution(mesh):
    return jax.shard_map(
        per_device,
        mesh=mesh,
        in_specs=(
            P(("dp", "tensor"), None),
            P(),
            P(None, "tensor"),
            P("tensor", None),
            P(("dp", "tensor"), None),
        ),
        out_specs=(
            P(("dp", "tensor"), None),
            P(("dp", "tensor"), None),
            P(None, "tensor"),
            P("tensor", None),
            P(),
        ),
        check_vma=False,
    )
```

time: 164 us -> 149 us (0.909)
  the two profiles are of different devices: /device:TPU:1 before, /device:TPU:33 now
where the time goes in v3:
time: 149 us
  Pallas kernels  140 us (94%)
  local copies, waits for them, and re-layouts  7.82 us (5%)
    pallas_call x1, Pallas kernels, per_device(): pl.pallas_call(kernel, out_shape=(pltpu.VMEM((R, D), BF16), pltpu.VMEM((R...  140 us
    unnamed x11, local copies, waits for them, and re-layouts  7.82 us

profile of v3, /device:TPU:33, one launch (start us, length us, event | category | flops | bytes accessed | tf_op | source)
XLA Modules:
  0.0 148.6 jit_solution(10275743364936798757)
XLA Ops:
  0.6 0.0 copy-start
  0.6 0.9 copy-done
  1.5 0.0 copy-start.1
  1.5 0.9 copy-done.1
  2.4 0.0 copy-start.2
  2.4 0.7 copy-done.2
  3.1 140.2 %shard_map.92 = (bf16[24,2560]{1,0:T(8,128)(2,1)S(1)}, bf16[24,2560]{1,0:T(8,128)(2,1)S(1)}, bf16[2560,640]{1,0:T(8,128)(2,1)S(1)}, bf16[640,2560]{1,0:T(8,128)(2,1)S(1)}, f32[20,128]{1,0:T(8,128)S(1)}) custom-call(bf16[24,2560]{1,0:T(8,128)(2,1)S(1)} %copy-done, f32[20,128]{1,0:T(8,128)S(1)} %bitcast.3, bf16[2560,640]{1,0:T(8,128)(2,1)} %wu_hbm.1, ...), custom_call_target="tpu_custom_call" | custom-call | tf_op jit(solution)/shard_map/pallas_call | solution.py:621
  143.3 0.7 copy.15
  144.0 0.6 copy.19
  144.6 0.6 copy.16
  145.2 1.7 %copy.17 = bf16[2560,640]{1,0:T(8,128)(2,1)} copy(bf16[2560,640]{1,0:T(8,128)(2,1)S(1)} %get-tuple-element.17) | data formatting | bytes 6553600
  146.9 1.7 %copy.18 = bf16[640,2560]{1,0:T(8,128)(2,1)} copy(bf16[640,2560]{1,0:T(8,128)(2,1)S(1)} %get-tuple-element.18) | data formatting | bytes 6553600
Async XLA Ops:
  0.6 0.9 copy-start
  1.5 0.9 copy-start.1
  2.4 0.7 copy-start.2

commit v4 on v3

--- a/solution.py
+++ b/solution.py
@@ -16,7 +16,7 @@
 T = 384
 R = 24
 H = D // 2
-N_SEND, N_RECV = 94, 143
+N_SEND, N_RECV = 95, 150
 
 SINE = (
     0.9999999958410793,
@@ -95,7 +95,7 @@
     out_ref, gin_ref, gup_ref, gdn_ref, gg_ref,
     x_ref, gain_ref, wu, wd, cg, qg, c2, aa, ss, cc, ghq, pa, gz2, hq, ht,
     po, px, ro, rx, zo, zx, w, wr, wz,
-    py, pz, gy, gzl, gx, gc, gh, gfull, mx, send, recv, local,
+    py, pz, gy, gzl, gx, gc, gh, xg, ig, gfull, mx, send, recv, local,
 ):
     dp, tn = lax.axis_index("dp"), lax.axis_index("tensor")
     zh, x, c = dp // 8, (dp // 2) % 4, dp % 2
@@ -141,6 +141,8 @@
     load_x.wait()
     wide = x_ref[...].astype(F32)
     inverse = lax.rsqrt(jnp.mean(wide * wide, axis=1, keepdims=True) + 1e-05)
+    ig[zl] = jnp.broadcast_to(inverse, (R, 128))
+    xg[zl] = x_ref[...]
     load_gain.wait()
     pl.semaphore_wait(barrier, len(peers))
 
@@ -206,6 +208,8 @@
     next_c(3)
     forward_q(2)
     next_c(2)
+    xz = [go(x_ref, xg.at[zl], peer) for peer in z_peers]
+    xz += [go(ig.at[zl], ig.at[zl], peer) for peer in z_peers]
 
     load_up.wait()
     near, last = (0, 12), (12, 4)
@@ -305,10 +309,6 @@
     load_own.wait()
     grad_group(near)
 
-    @pl.loop(0, 5)
-    def _(i):
-        lay(i, c * H, put_own)
-
     for copy in pyx:
         copy.wait_recv()
     peak = jnp.maximum(jnp.maximum(py[0], py[1]), jnp.maximum(py[2], py[3]))
@@ -317,6 +317,11 @@
     for copy in cf:
         copy.wait_recv()
     grad_group(last)
+
+    @pl.loop(0, 5)
+    def _(i):
+        lay(i, c * H, put_own)
+
 
     class Ring:
         def __init__(self, plus, minus, view, got, tiles, cut):
@@ -352,10 +357,11 @@
             )
 
         def cross_z(self):
-            self.far = go(w.at[self.n, x], wz.at[self.n], zfar)
+            self.far = [go(w.at[self.n, x], wz.at[self.n], zfar)]
 
         def begin(self):
-            self.far.wait_recv()
+            for copy in self.far:
+                copy.wait_recv()
             for way in (0, 1):
                 both = w[self.n, x, way].astype(F32) + wz[self.n, way].astype(F32)
                 self.buf[self.where(c, x, way)] = both.astype(BF16)
@@ -387,6 +393,31 @@
             for copy in self.cross:
                 copy.wait_recv()
 
+    class First(Part):
+        def __init__(self, *args):
+            super().__init__(*args)
+            self.got, self.far = [None, None], []
+
+        def send(self, half):
+            self.got[half] = [
+                go(w.at[self.n, mod(x + k), half], wr.at[self.n, half, k - 1], x_peers[k - 1])
+                for k in (1, 3, 2)
+            ]
+
+        def take(self, half):
+            for copy in self.got[half]:
+                copy.wait_recv()
+            mine, got = w.at[self.n, x, half], wr.at[self.n, half]
+
+            @pl.loop(0, 5)
+            def _(i):
+                at = pl.ds(pl.multiple_of(i * 16, 16), 16)
+                t = mine[at].astype(F32) + got[0, at].astype(F32)
+                t = t + got[1, at].astype(F32) + got[2, at].astype(F32)
+                mine[at] = t.astype(BF16)
+
+            self.far.append(go(mine, wz.at[self.n, half], zfar))
+
     def up_rows(p):
         def where(core, j, way=None):
             start = core * H + j * 320 + p * 160 + (0 if way is None else way * 80)
@@ -404,7 +435,7 @@
 
         return where
 
-    j1, j2 = Part(0, gup_ref, up_rows(0)), Part(1, gup_ref, up_rows(1))
+    j1, j2 = First(0, gup_ref, up_rows(0)), Part(1, gup_ref, up_rows(1))
     j3, j4 = Part(2, gdn_ref, down_rows(0)), Part(3, gdn_ref, down_rows(1))
 
     def p_view(buf):
@@ -422,11 +453,16 @@
         w[p, j] = dot(aa[rows, :], gz2[...]).reshape(2, 80, F).astype(BF16)
 
     mark = len(copies.open)
-    up_chunk(0, mod(x - 1))
-    j1.ring.send(0, 0)
-    up_chunk(0, mod(x + 1))
-    j1.ring.send(0, 1)
-    up_chunk(0, mod(x + 2))
+    def up_half(half):
+        for k in (1, 3, 2, 0):
+            j = mod(x + k)
+            rows = pl.ds(pl.multiple_of(j * 320 + half * 80, 16), 80)
+            w[0, j, half] = dot(aa[rows, :], gz2[...]).astype(BF16)
+
+    up_half(0)
+    j1.send(0)
+    up_half(1)
+    j1.send(1)
 
     @pl.loop(0, 5)
     def _(i):
@@ -436,9 +472,10 @@
 
     gin.send(0, 0)
     gin.send(0, 1)
-    j1.ring.take(0)
-    up_chunk(0, x)
-    copies.sent(mark)
+    up_chunk(1, mod(x - 1))
+    j2.ring.send(0, 0)
+    up_chunk(1, mod(x + 1))
+    j2.ring.send(0, 1)
 
     for copy in pzx:
         copy.wait_recv()
@@ -460,17 +497,10 @@
             hq[rows, cols] = q.T.astype(BF16)
 
     hidden_tile(0)
-    up_chunk(1, mod(x - 1))
-    up_chunk(1, mod(x + 1))
-    j1.ring.take(1)
-    j2.ring.send(0, 0)
-    j2.ring.send(0, 1)
     hidden_tile(1)
-    up_chunk(1, mod(x + 2))
-    up_chunk(1, x)
+    j1.take(0)
     hidden_tile(2)
     htx = go(ht.at[:, pl.ds(0, T)], ht.at[:, pl.ds(T, T)], other)
-    gin.take(0)
 
     def down_chunk(j):
         rows = pl.ds(pl.multiple_of(j * 160, 160), 160)
@@ -478,10 +508,9 @@
             part = dot(ht[rows, :], cc[:, p * F : (p + 1) * F])
             w[2 + p, j] = part.reshape(2, 80, F).astype(BF16)
 
-    j1.ring.take(2)
-    j1.cross_z()
-    j2.ring.take(0)
+    up_chunk(1, mod(x + 2))
     cc[pl.ds(0, T), :] = c2[:, own_half]
+    copies.sent(mark)
     for copy in ccx:
         copy.wait_recv()
     htx.wait_recv()
@@ -489,8 +518,12 @@
     j3.ring.send(0, 0)
     down_chunk(mod(x + 1))
     j3.ring.send(0, 1)
-    j2.ring.take(1)
-    gin.take(1)
+    j2.ring.take(0)
+    j1.take(1)
+    gin.take(0)
+    j4.ring.send(0, 0)
+    j4.ring.send(0, 1)
+    up_chunk(1, x)
     down_chunk(mod(x + 2))
     down_chunk(x)
 
@@ -500,13 +533,11 @@
         po[:, :, :, ns] = part.reshape(4, 4, R, 512).astype(BF16)
 
     out_tile(0)
-    j2.ring.take(2)
-    j2.cross_z()
-    j4.ring.send(0, 0)
-    j4.ring.send(0, 1)
+    j2.ring.take(1)
     out_tile(1)
     j3.ring.take(0)
     out_tile(2)
+    gin.take(1)
     out_tile(3)
     out_tile(4)
     out.send(0, 0)
@@ -517,25 +548,57 @@
             go(buf.at[place(0), mod(zl + k)], got.at[k - 1], z_peers[k - 1]) for k in (1, 2, 3)
         ]
 
+    j2.ring.take(2)
+    j2.cross_z()
+    j4.ring.take(0)
+    j3.ring.take(1)
     gin.take(2)
     gin_z = scatter_z(px, zx)
-    j3.ring.take(1)
-    j4.ring.take(0)
+
+    for copy in xz:
+        copy.wait_recv()
+    for i in range(D // 128):
+        cols = slice(i * 128, (i + 1) * 128)
+        t = jnp.zeros((R, 128), F32)
+        for k in range(4):
+            g = px[place(0), k, :, cols].astype(F32)
+            t = t + g * xg[k, :, cols].astype(F32) * ig[k]
+        gy[y, i : i + 1, :] = jnp.sum(t, axis=0, keepdims=True)
+    gyx = [go(gy.at[y], gy.at[y], peer) for peer in y_peers]
+
     j1.begin()
+    j4.ring.take(1)
     j3.ring.take(2)
     j3.cross_z()
-    j4.ring.take(1)
+    for copy in gyx:
+        copy.wait_recv()
+    gx[x] = gy[0] + gy[1] + gy[2] + gy[3]
+    gxx = [go(gx.at[x], gx.at[x], peer) for peer in x_peers]
     out.take(0)
+    j1.middle()
     j4.ring.take(2)
     j4.cross_z()
-    j1.middle()
     j2.begin()
+    j1.end()
     out.take(1)
-    j1.end()
     j2.middle()
     out.take(2)
+    for copy in gxx:
+        copy.wait_recv()
+    gc[c] = gx[0] + gx[1] + gx[2] + gx[3]
+    gcx = go(gc.at[c], gc.at[c], other)
+    j2.end()
+    gcx.wait_recv()
+    gzl[zl] = gc[0] + gc[1]
+    gzx2 = [go(gzl.at[zl], gzl.at[zl], peer) for peer in z_peers]
+    j3.begin()
+    j3.middle()
+    j4.begin()
+    for copy in gzx2:
+        copy.wait_recv()
+    gh[zh] = gzl[0] + gzl[1] + gzl[2] + gzl[3]
+    ghx = go(gh.at[zh], gh.at[zh], zfar)
     out_z = scatter_z(po, zo)
-    j2.end()
 
     for copy in gin_z:
         copy.wait_recv()
@@ -551,9 +614,7 @@
         t = x_ref[:, cols].astype(F32)
         gfull[:, cols] = g
         dots = dots + g * gain_ref[i : i + 1, :] * t
-        gy[y, i : i + 1, :] = jnp.sum(g * t * inverse, axis=0, keepdims=True)
-    gyx = [go(gy.at[y], gy.at[y], peer) for peer in y_peers]
-    j3.begin()
+    j3.end()
     mean = jnp.sum(dots, axis=1, keepdims=True) * (1.0 / D)
     cubed = inverse * inverse * inverse * mean
     for i in range(D // 128):
@@ -563,25 +624,8 @@
             inverse * (gfull[:, cols] * gain_ref[i : i + 1, :]) - t * cubed
         ).astype(BF16)
 
-    for copy in gyx:
-        copy.wait_recv()
-    gzl[zl] = gy[0] + gy[1] + gy[2] + gy[3]
-    gzx2 = [go(gzl.at[zl], gzl.at[zl], peer) for peer in z_peers]
-    j3.middle()
-    j4.begin()
-    for copy in gzx2:
-        copy.wait_recv()
-    gx[x] = gzl[0] + gzl[1] + gzl[2] + gzl[3]
-    gxx = [go(gx.at[x], gx.at[x], peer) for peer in x_peers]
-    j3.end()
-    for copy in gxx:
-        copy.wait_recv()
-    gc[c] = gx[0] + gx[1] + gx[2] + gx[3]
-    gcx = go(gc.at[c], gc.at[c], other)
     j4.middle()
-    gcx.wait_recv()
-    gh[zh] = gc[0] + gc[1]
-    ghx = go(gh.at[zh], gh.at[zh], zfar)
+    j4.end()
 
     for copy in out_z:
         copy.wait_recv()
@@ -589,7 +633,6 @@
         cols = slice(i * 128, (i + 1) * 128)
         out_ref[:, cols] = total(po, zo, cols).astype(BF16)
 
-    j4.end()
     ghx.wait_recv()
     gg_ref[...] = gh[0] + gh[1]
     for part in (j1, j2, j3, j4):
@@ -616,6 +659,7 @@
         ((4, 8, 128), F32), ((4, 8, 128), F32),
         ((4, 20, 128), F32), ((4, 20, 128), F32), ((4, 20, 128), F32),
         ((2, 20, 128), F32), ((2, 20, 128), F32),
+        ((4, R, D), BF16), ((4, R, 128), F32),
         ((R, D), F32), ((R, 128), F32),
     ]
     out, gin, gup, gdn, gg = pl.pallas_call(

time: 149 us -> 138 us (0.926)
  the two profiles are of different devices: /device:TPU:33 before, /device:TPU:1 now
where the time goes in v4:
time: 138 us; the launch traced here: 137 us
  Pallas kernels  129 us (93%)
  local copies, waits for them, and re-layouts  7.82 us (6%)
    pallas_call x1, Pallas kernels, per_device(): pl.pallas_call(kernel, out_shape=(pltpu.VMEM((R, D), BF16), pltpu.VMEM((R...  129 us
    unnamed x11, local copies, waits for them, and re-layouts  7.82 us

profile of v4, /device:TPU:1, one launch (start us, length us, event | category | flops | bytes accessed | tf_op | source)
XLA Modules:
  0.0 137.4 jit_solution(7482173755691458100)
XLA Ops:
  0.6 0.0 copy-start
  0.6 0.9 copy-done
  1.5 0.0 copy-start.1
  1.5 0.9 copy-done.1
  2.4 0.0 copy-start.2
  2.4 0.7 copy-done.2
  3.1 128.9 %shard_map.92 = (bf16[24,2560]{1,0:T(8,128)(2,1)S(1)}, bf16[24,2560]{1,0:T(8,128)(2,1)S(1)}, bf16[2560,640]{1,0:T(8,128)(2,1)S(1)}, bf16[640,2560]{1,0:T(8,128)(2,1)S(1)}, f32[20,128]{1,0:T(8,128)S(1)}) custom-call(bf16[24,2560]{1,0:T(8,128)(2,1)S(1)} %copy-done, f32[20,128]{1,0:T(8,128)S(1)} %bitcast.3, bf16[2560,640]{1,0:T(8,128)(2,1)} %wu_hbm.1, ...), custom_call_target="tpu_custom_call" | custom-call | tf_op jit(solution)/shard_map/pallas_call | solution.py:665
  132.1 0.7 copy.15
  132.7 0.6 copy.19
  133.3 0.6 copy.16
  134.0 1.7 %copy.17 = bf16[2560,640]{1,0:T(8,128)(2,1)} copy(bf16[2560,640]{1,0:T(8,128)(2,1)S(1)} %get-tuple-element.17) | data formatting | bytes 6553600
  135.7 1.7 %copy.18 = bf16[640,2560]{1,0:T(8,128)(2,1)} copy(bf16[640,2560]{1,0:T(8,128)(2,1)S(1)} %get-tuple-element.18) | data formatting | bytes 6553600
Async XLA Ops:
  0.6 0.9 copy-start
  1.5 0.9 copy-start.1
  2.4 0.7 copy-start.2

commit v5 on v4

--- a/solution.py
+++ b/solution.py
@@ -16,7 +16,7 @@
 T = 384
 R = 24
 H = D // 2
-N_SEND, N_RECV = 95, 150
+N_SEND, N_RECV = 96, 151
 
 SINE = (
     0.9999999958410793,
@@ -435,7 +435,7 @@
 
         return where
 
-    j1, j2 = First(0, gup_ref, up_rows(0)), Part(1, gup_ref, up_rows(1))
+    j1, j2 = First(0, gup_ref, up_rows(0)), First(1, gup_ref, up_rows(1))
     j3, j4 = Part(2, gdn_ref, down_rows(0)), Part(3, gdn_ref, down_rows(1))
 
     def p_view(buf):
@@ -472,10 +472,10 @@
 
     gin.send(0, 0)
     gin.send(0, 1)
-    up_chunk(1, mod(x - 1))
-    j2.ring.send(0, 0)
-    up_chunk(1, mod(x + 1))
-    j2.ring.send(0, 1)
+    for k in (1, 3, 2):
+        up_chunk(1, mod(x + k))
+    j2.send(0)
+    j2.send(1)
 
     for copy in pzx:
         copy.wait_recv()
@@ -508,9 +508,10 @@
             part = dot(ht[rows, :], cc[:, p * F : (p + 1) * F])
             w[2 + p, j] = part.reshape(2, 80, F).astype(BF16)
 
-    up_chunk(1, mod(x + 2))
+    up_chunk(1, x)
     cc[pl.ds(0, T), :] = c2[:, own_half]
     copies.sent(mark)
+    gin.take(0)
     for copy in ccx:
         copy.wait_recv()
     htx.wait_recv()
@@ -518,12 +519,9 @@
     j3.ring.send(0, 0)
     down_chunk(mod(x + 1))
     j3.ring.send(0, 1)
-    j2.ring.take(0)
     j1.take(1)
-    gin.take(0)
     j4.ring.send(0, 0)
     j4.ring.send(0, 1)
-    up_chunk(1, x)
     down_chunk(mod(x + 2))
     down_chunk(x)
 
@@ -533,27 +531,49 @@
         po[:, :, :, ns] = part.reshape(4, 4, R, 512).astype(BF16)
 
     out_tile(0)
-    j2.ring.take(1)
+    j2.take(0)
     out_tile(1)
-    j3.ring.take(0)
+    gin.take(1)
     out_tile(2)
-    gin.take(1)
     out_tile(3)
     out_tile(4)
     out.send(0, 0)
     out.send(0, 1)
 
-    def scatter_z(buf, got):
-        return [
-            go(buf.at[place(0), mod(zl + k)], got.at[k - 1], z_peers[k - 1]) for k in (1, 2, 3)
-        ]
-
-    j2.ring.take(2)
-    j2.cross_z()
+    class ScatterZ:
+        def __init__(self, buf, got):
+            self.buf, self.got = buf.at[place(0)], got
+            near = zl + 1 - 2 * lax.rem(zl, 2)
+            self.across = mod(zl + 2)
+            self.near = [
+                go(self.buf.at[mod(near + 2)], got.at[1], dev(zl=near)),
+                go(self.buf.at[near], got.at[0], dev(zl=near)),
+            ]
+
+        def middle(self):
+            self.near[0].wait_recv()
+            mine = self.buf.at[self.across]
+
+            @pl.loop(0, 5)
+            def _(i):
+                cols = pl.ds(pl.multiple_of(i * 512, 512), 512)
+                t = mine[:, cols].astype(F32) + self.got[1, :, cols].astype(F32)
+                mine[:, cols] = t.astype(BF16)
+
+            self.far = go(mine, self.got.at[2], dev(zl=self.across))
+
+        def end(self):
+            self.near[1].wait_recv()
+            self.far.wait_recv()
+
+        def total(self, cols):
+            t = self.buf[zl, :, cols].astype(F32) + self.got[0, :, cols].astype(F32)
+            return t + self.got[2, :, cols].astype(F32)
+
+    j2.take(1)
+    j3.ring.take(0)
     j4.ring.take(0)
-    j3.ring.take(1)
     gin.take(2)
-    gin_z = scatter_z(px, zx)
 
     for copy in xz:
         copy.wait_recv()
@@ -563,58 +583,58 @@
         for k in range(4):
             g = px[place(0), k, :, cols].astype(F32)
             t = t + g * xg[k, :, cols].astype(F32) * ig[k]
-        gy[y, i : i + 1, :] = jnp.sum(t, axis=0, keepdims=True)
-    gyx = [go(gy.at[y], gy.at[y], peer) for peer in y_peers]
-
+        gzl[zl, i : i + 1, :] = jnp.sum(t, axis=0, keepdims=True)
+    gain_copies = [go(gzl.at[zl], gzl.at[zl], peer) for peer in z_peers]
+    gin_z = ScatterZ(px, zx)
+
+    def gain_sum(parts, n, nxt, at, to):
+        for copy in gain_copies:
+            copy.wait_recv()
+        t = parts[0]
+        for k in range(1, n):
+            t = t + parts[k]
+        if nxt is not None:
+            nxt[at] = t
+            gain_copies[:] = [go(nxt.at[at], nxt.at[at], peer) for peer in to]
+        return t
+
+    j3.ring.take(1)
     j1.begin()
+    out.take(0)
     j4.ring.take(1)
     j3.ring.take(2)
     j3.cross_z()
-    for copy in gyx:
-        copy.wait_recv()
-    gx[x] = gy[0] + gy[1] + gy[2] + gy[3]
-    gxx = [go(gx.at[x], gx.at[x], peer) for peer in x_peers]
-    out.take(0)
     j1.middle()
     j4.ring.take(2)
     j4.cross_z()
     j2.begin()
     j1.end()
     out.take(1)
+    gain_sum(gzl, 4, gy, y, y_peers)
+    gin_z.middle()
     j2.middle()
     out.take(2)
-    for copy in gxx:
-        copy.wait_recv()
-    gc[c] = gx[0] + gx[1] + gx[2] + gx[3]
-    gcx = go(gc.at[c], gc.at[c], other)
+    j3.begin()
+    gain_sum(gy, 4, gx, x, x_peers)
     j2.end()
-    gcx.wait_recv()
-    gzl[zl] = gc[0] + gc[1]
-    gzx2 = [go(gzl.at[zl], gzl.at[zl], peer) for peer in z_peers]
-    j3.begin()
+    j4.begin()
+    out_z = ScatterZ(po, zo)
     j3.middle()
-    j4.begin()
-    for copy in gzx2:
-        copy.wait_recv()
-    gh[zh] = gzl[0] + gzl[1] + gzl[2] + gzl[3]
-    ghx = go(gh.at[zh], gh.at[zh], zfar)
-    out_z = scatter_z(po, zo)
-
-    for copy in gin_z:
-        copy.wait_recv()
-
-    def total(buf, got, cols):
-        t = buf[place(0), zl, :, cols].astype(F32) + got[0, :, cols].astype(F32)
-        return t + got[1, :, cols].astype(F32) + got[2, :, cols].astype(F32)
+    gain_sum(gx, 4, gc, c, [other])
+    j3.end()
+    gain_sum(gc, 2, gh, zh, [zfar])
+    j4.middle()
+    out_z.middle()
+
+    gin_z.end()
 
     dots = jnp.zeros((R, 128), F32)
     for i in range(D // 128):
         cols = slice(i * 128, (i + 1) * 128)
-        g = total(px, zx, cols)
+        g = gin_z.total(cols)
         t = x_ref[:, cols].astype(F32)
         gfull[:, cols] = g
         dots = dots + g * gain_ref[i : i + 1, :] * t
-    j3.end()
     mean = jnp.sum(dots, axis=1, keepdims=True) * (1.0 / D)
     cubed = inverse * inverse * inverse * mean
     for i in range(D // 128):
@@ -624,17 +644,14 @@
             inverse * (gfull[:, cols] * gain_ref[i : i + 1, :]) - t * cubed
         ).astype(BF16)
 
-    j4.middle()
     j4.end()
 
-    for copy in out_z:
-        copy.wait_recv()
+    out_z.end()
     for i in range(D // 128):
         cols = slice(i * 128, (i + 1) * 128)
-        out_ref[:, cols] = total(po, zo, cols).astype(BF16)
-
-    ghx.wait_recv()
-    gg_ref[...] = gh[0] + gh[1]
+        out_ref[:, cols] = out_z.total(cols).astype(BF16)
+
+    gg_ref[...] = gain_sum(gh, 2, None, None, None)
     for part in (j1, j2, j3, j4):
         part.finish()
     copies.sent()
@@ -662,17 +679,13 @@
         ((4, R, D), BF16), ((4, R, 128), F32),
         ((R, D), F32), ((R, 128), F32),
     ]
+    shapes = [(R, D), (R, D), (D, F), (F, D), (D // 128, 128)]
+    types = [BF16, BF16, BF16, BF16, F32]
     out, gin, gup, gdn, gg = pl.pallas_call(
         kernel,
-        out_shape=(
-            pltpu.VMEM((R, D), BF16),
-            pltpu.VMEM((R, D), BF16),
-            pltpu.VMEM((D, F), BF16),
-            pltpu.VMEM((F, D), BF16),
-            pltpu.VMEM((D // 128, 128), F32),
-        ),
+        out_shape=[pltpu.VMEM(s, t) for s, t in zip(shapes, types, strict=True)],
         in_specs=[hbm] * 5,
-        out_specs=(vmem,) * 5,
+        out_specs=[vmem] * 5,
         scratch_shapes=[pltpu.VMEM(s, t) for s, t in scratch]
         + [
             pltpu.SemaphoreType.DMA((N_SEND,)),

time: 138 us -> 128 us (0.928)
  Pallas kernels: 129 us -> 119 us
    pallas_call x1, Pallas kernels: 129 us -> 119 us  [per_device(): pl.pallas_call(kernel, out_shape=[pltpu.VMEM(s, t) for s, t in zip(shapes...]
where the time goes in v5:
time: 128 us
  Pallas kernels  119 us (93%)
  local copies, waits for them, and re-layouts  7.82 us (6%)
    pallas_call x1, Pallas kernels, per_device(): pl.pallas_call(kernel, out_shape=[pltpu.VMEM(s, t) for s, t in zip(shapes...  119 us
    unnamed x11, local copies, waits for them, and re-layouts  7.82 us

profile of v5, /device:TPU:1, one launch (start us, length us, event | category | flops | bytes accessed | tf_op | source)
XLA Modules:
  0.0 127.6 jit_solution(12982297739733983964)
XLA Ops:
  0.6 0.0 copy-start
  0.6 0.9 copy-done
  1.5 0.0 copy-start.1
  1.5 0.9 copy-done.1
  2.4 0.0 copy-start.2
  2.4 0.7 copy-done.2
  3.1 119.2 %shard_map.92 = (bf16[24,2560]{1,0:T(8,128)(2,1)S(1)}, bf16[24,2560]{1,0:T(8,128)(2,1)S(1)}, bf16[2560,640]{1,0:T(8,128)(2,1)S(1)}, bf16[640,2560]{1,0:T(8,128)(2,1)S(1)}, f32[20,128]{1,0:T(8,128)S(1)}) custom-call(bf16[24,2560]{1,0:T(8,128)(2,1)S(1)} %copy-done, f32[20,128]{1,0:T(8,128)S(1)} %bitcast.3, bf16[2560,640]{1,0:T(8,128)(2,1)} %wu_hbm.1, ...), custom_call_target="tpu_custom_call" | custom-call | tf_op jit(solution)/shard_map/pallas_call | solution.py:684
  122.3 0.7 copy.15
  123.0 0.6 copy.19
  123.6 0.6 copy.16
  124.2 1.7 %copy.17 = bf16[2560,640]{1,0:T(8,128)(2,1)} copy(bf16[2560,640]{1,0:T(8,128)(2,1)S(1)} %get-tuple-element.17) | data formatting | bytes 6553600
  125.9 1.7 %copy.18 = bf16[640,2560]{1,0:T(8,128)(2,1)} copy(bf16[640,2560]{1,0:T(8,128)(2,1)S(1)} %get-tuple-element.18) | data formatting | bytes 6553600
Async XLA Ops:
  0.6 0.9 copy-start
  1.5 0.9 copy-start.1
  2.4 0.7 copy-start.2

commit v6 on v5

--- a/solution.py
+++ b/solution.py
@@ -693,7 +693,7 @@
             pltpu.SemaphoreType.DMA((5,)),
         ],
         compiler_params=pltpu.CompilerParams(
-            collective_id=0, has_side_effects=True, vmem_limit_bytes=46 << 20
+            collective_id=0, has_side_effects=True, vmem_limit_bytes=60231680
         ),
     )(inputs, norm_gain.reshape(D // 128, 128), w_up, w_down, grad_out)
     return out, gin, gup, gdn, gg.reshape(D)

time: 128 us -> 125 us (0.977)
  local copies, waits for them, and re-layouts: 7.82 us -> 5.31 us
    unnamed x11 -> x5, local copies, waits for them, and re-layouts: 7.82 us -> 5.31 us
where the time goes in v6:
time: 125 us
  Pallas kernels  119 us (95%)
  local copies, waits for them, and re-layouts  5.31 us (4%)
    pallas_call x1, Pallas kernels, per_device(): pl.pallas_call(kernel, out_shape=[pltpu.VMEM(s, t) for s, t in zip(shapes...  119 us
    unnamed x5, local copies, waits for them, and re-layouts  5.31 us

profile of v6, /device:TPU:1, one launch (start us, length us, event | category | flops | bytes accessed | tf_op | source)
XLA Modules:
  0.0 125.0 jit_solution(13201109502440779681)
XLA Ops:
  0.6 119.0 %shard_map.92 = (bf16[24,2560]{1,0:T(8,128)(2,1)S(1)}, bf16[24,2560]{1,0:T(8,128)(2,1)S(1)}, bf16[2560,640]{1,0:T(8,128)(2,1)S(1)}, bf16[640,2560]{1,0:T(8,128)(2,1)S(1)}, f32[20,128]{1,0:T(8,128)S(1)}) custom-call(bf16[24,2560]{1,0:T(8,128)(2,1)} %x_hbm.1, f32[20,128]{1,0:T(8,128)} %bitcast.3, bf16[2560,640]{1,0:T(8,128)(2,1)} %wu_hbm.1, ...), custom_call_target="tpu_custom_call" | custom-call | tf_op jit(solution)/shard_map/pallas_call | solution.py:684
  119.7 0.7 copy.15
  120.3 0.6 copy.19
  120.9 0.6 copy.16
  121.6 1.7 %copy.17 = bf16[2560,640]{1,0:T(8,128)(2,1)} copy(bf16[2560,640]{1,0:T(8,128)(2,1)S(1)} %get-tuple-element.17) | data formatting | bytes 6553600
  123.3 1.7 %copy.18 = bf16[640,2560]{1,0:T(8,128)(2,1)} copy(bf16[640,2560]{1,0:T(8,128)(2,1)S(1)} %get-tuple-element.18) | data formatting | bytes 6553600

commit v7 on v6

--- a/solution.py
+++ b/solution.py
@@ -245,6 +245,25 @@
 
     mx[...] = jnp.zeros((R, 128), F32)
     pre_group(near, mx)
+
+    def lay(part, far):
+        blocks = slice(0, 11) if part == 0 else slice(10, 16)
+        keep = slice(0, 256) if part == 0 else slice(16, 144)
+        lanes = slice(0, 256) if part == 0 else slice(256, T)
+        start = (1 - c) * H if far else c * H
+
+        @pl.loop(0, 5)
+        def _(i):
+            cols = pl.ds(pl.multiple_of(start + i * 256, 256), 256)
+            rows = pl.ds(pl.multiple_of(i * 256, 256), 256)
+            v = qg[blocks, :, cols].astype(F32).reshape(-1, 256)[keep].T.astype(BF16)
+            if far:
+                ss[rows, lanes] = v
+            else:
+                aa[rows, lanes] = v
+
+    lay(0, True)
+    lay(0, False)
     for copy in qf:
         copy.wait_recv()
     forward_c(3)
@@ -254,21 +273,7 @@
     pyx = [go(py.at[y], py.at[y], peer) for peer in y_peers]
     forward_c(2)
 
-    def lay(i, start, put):
-        cols = pl.ds(pl.multiple_of(start + i * 256, 256), 256)
-        v = qg[:, :, cols].astype(F32).reshape(T, 256)
-        put(pl.ds(pl.multiple_of(i * 256, 256), 256), v.T.astype(BF16))
-
-    def put_other(rows, v):
-        ss[rows, :] = v
-
-    def put_own(rows, v):
-        aa[rows, pl.ds(0, T)] = v
-
-    @pl.loop(0, 5)
-    def _(i):
-        lay(i, (1 - c) * H, put_other)
-
+    lay(1, True)
     aax = go(ss, aa.at[:, pl.ds(T, T)], other)
 
     load_down.wait()
@@ -318,9 +323,7 @@
         copy.wait_recv()
     grad_group(last)
 
-    @pl.loop(0, 5)
-    def _(i):
-        lay(i, c * H, put_own)
+    lay(1, False)
 
 
     class Ring:
@@ -621,10 +624,10 @@
     out_z = ScatterZ(po, zo)
     j3.middle()
     gain_sum(gx, 4, gc, c, [other])
+    j4.middle()
+    gain_sum(gc, 2, gh, zh, [zfar])
+    out_z.middle()
     j3.end()
-    gain_sum(gc, 2, gh, zh, [zfar])
-    j4.middle()
-    out_z.middle()
 
     gin_z.end()
 

time: 125 us -> 124 us (level)
    pallas_call x1, Pallas kernels: 119 us -> 118 us  [per_device(): pl.pallas_call(kernel, out_shape=[pltpu.VMEM(s, t) for s, t in zip(shapes...]
where the time goes in v7:
time: 124 us
  Pallas kernels  118 us (95%)
  local copies, waits for them, and re-layouts  5.31 us (4%)
    pallas_call x1, Pallas kernels, per_device(): pl.pallas_call(kernel, out_shape=[pltpu.VMEM(s, t) for s, t in zip(shapes...  118 us
    unnamed x5, local copies, waits for them, and re-layouts  5.31 us

profile of v7, /device:TPU:1, one launch (start us, length us, event | category | flops | bytes accessed | tf_op | source)
XLA Modules:
  0.0 123.6 jit_solution(14095614075351345705)
XLA Ops:
  0.6 117.7 %shard_map.92 = (bf16[24,2560]{1,0:T(8,128)(2,1)S(1)}, bf16[24,2560]{1,0:T(8,128)(2,1)S(1)}, bf16[2560,640]{1,0:T(8,128)(2,1)S(1)}, bf16[640,2560]{1,0:T(8,128)(2,1)S(1)}, f32[20,128]{1,0:T(8,128)S(1)}) custom-call(bf16[24,2560]{1,0:T(8,128)(2,1)} %x_hbm.1, f32[20,128]{1,0:T(8,128)} %bitcast.3, bf16[2560,640]{1,0:T(8,128)(2,1)} %wu_hbm.1, ...), custom_call_target="tpu_custom_call" | custom-call | tf_op jit(solution)/shard_map/pallas_call | solution.py:687
  118.3 0.7 copy.15
  119.0 0.6 copy.19
  119.6 0.6 copy.16
  120.2 1.7 %copy.17 = bf16[2560,640]{1,0:T(8,128)(2,1)} copy(bf16[2560,640]{1,0:T(8,128)(2,1)S(1)} %get-tuple-element.17) | data formatting | bytes 6553600
  121.9 1.7 %copy.18 = bf16[640,2560]{1,0:T(8,128)(2,1)} copy(bf16[640,2560]{1,0:T(8,128)(2,1)S(1)} %get-tuple-element.18) | data formatting | bytes 6553600
